TPU v7x, 256 devices: a whole 4x4x8 slice. The times are simulated.
256 devices in a mesh: section: 16 (over z, core), req: 16 (over y, x).
Axes of the slice: x: 4, y: 4, z: 8, core: 2. Of those that a mesh axis runs over, the one named last changes fastest.
Arguments:
- latents: bfloat16 [128, 3072], P('req'), may hold values from -6 to 6
- patch_route: int32 [128], replicated, may hold values from 0 to 127, each once
- request_len: int32 [16], replicated, may hold values from 1 to 32, 128 in all
- span_order: int32 [2], replicated, may hold values from 0 to 1, each once
- modulation: float32 [16, 16, 3, 3072], P('section'), may hold values from -4 to 4
- w_qkv: bfloat16 [16, 3072, 16, 384], P('section', None, 'req'), may hold values from -0.109375 to 0.109375
- w_mlp_in: bfloat16 [16, 3072, 6144], P('section', None, 'req'), may hold values from -0.109375 to 0.109375
- w_out_attn: bfloat16 [16, 16, 128, 3072], P('section', 'req'), may hold values from -0.0625 to 0.0625
- w_out_mlp: bfloat16 [16, 6144, 3072], P('section', 'req'), may hold values from -0.0625 to 0.0625
- stale_kv: bfloat16 [16, 128, 16, 256], P('section', None, 'req'), may hold values from -160 to 160
Outputs:
- denoised: bfloat16 [128, 3072], P('req', 'section')
All inputs are finite; a program needn't handle non-finite values.
Results may differ from a plain program's by a relative error of at most 0.04.
Values may be sent and summed in bfloat16 or wider, within the bound.
No kernel may reach another device: no remote copies, remote signals or barrier semaphores. Data moves between devices by JAX's collectives and lax.ppermute only.
A program may use at most 64 MiB of HBM per device.

v0:
```python
import jax
import jax.numpy as jnp
from jax import lax
from jax.sharding import PartitionSpec as P


def from_behind(block, axis, distance):
    devices = range(lax.axis_size(axis))
    route = [(i - distance, i) for i in devices if i - distance in devices]
    return lax.ppermute(block, axis, route)


def spread_2(value, axis, source):
    kept = jnp.where(lax.axis_index(axis) == source, value, 0).astype(value.dtype)
    return lax.psum(kept, axis)


def layer_norm(values):
    row_mean = jnp.mean(values, axis=-1, keepdims=True)
    centered = values - row_mean
    row_var = jnp.mean(centered * centered, axis=-1, keepdims=True)
    return centered * lax.rsqrt(row_var + 1e-06)


def gelu_tanh(values):
    return (
        0.5
        * values
        * (1.0 + jnp.tanh(0.7978845608028654 * (values + 0.044715 * values * values * values)))
    )


def shards(
    latents,
    patch_route,
    request_len,
    span_order,
    modulation,
    w_qkv,
    w_mlp_in,
    w_out_attn,
    w_out_mlp,
    stale_kv,
):
    section_count = lax.axis_size("section")
    req_count = lax.axis_size("req")
    section_index = lax.axis_index("section")
    req_index = lax.axis_index("req")
    patches = patch_route.shape[0]
    span_count = span_order.shape[0]
    span_rows = patches // span_count
    model_width = latents.shape[1]
    col_width = model_width // req_count
    section_cols = model_width // section_count
    req_total = request_len.shape[0]
    heads_dev = w_qkv.shape[2]
    head_dim = w_qkv.shape[3] // 3
    starts = jnp.cumsum(request_len) - request_len
    patch_ids = jnp.arange(patches, dtype=jnp.int32)
    owner_req = jnp.sum((patch_ids[:, None] >= starts[None, :]).astype(jnp.int32), axis=1) - 1
    seq_req = owner_req[patch_route]
    req_ids = jnp.arange(req_total, dtype=jnp.int32)
    mod_table = modulation[0].reshape(req_total, 3 * model_width)
    qkv_weight = w_qkv[0].reshape(model_width, heads_dev * 3 * head_dim)
    mlp_weight = w_mlp_in[0]
    attn_out_weight = w_out_attn[0].reshape(heads_dev * head_dim, model_width)
    mlp_out_weight = w_out_mlp[0]
    spread = lax.all_to_all(latents, "req", split_axis=1, concat_axis=0, tiled=True)
    sequence = spread[patch_route]
    in_width = sequence.shape[1]

    def work(incoming, kv_cache, span_id):
        first_row = span_id * span_rows
        row_req = lax.dynamic_slice_in_dim(seq_req, first_row, span_rows, 0)
        onehot = (row_req[:, None] == req_ids[None, :]).astype(jnp.float32)
        mod_rows = jnp.dot(onehot, mod_table, precision=lax.Precision.HIGHEST).reshape(
            span_rows, 3, model_width
        )
        current = lax.all_gather(incoming, "req", axis=1, tiled=True)
        normed = (
            layer_norm(current.astype(jnp.float32)) * (1.0 + mod_rows[:, 1]) + mod_rows[:, 0]
        ).astype(jnp.bfloat16)
        qkv_rows = jnp.dot(normed, qkv_weight, preferred_element_type=jnp.float32).reshape(
            span_rows, heads_dev, 3 * head_dim
        )
        query_rows = qkv_rows[:, :, :head_dim].astype(jnp.bfloat16)
        fresh_kv = qkv_rows[:, :, head_dim:].astype(jnp.bfloat16)
        kv_cache = lax.dynamic_update_slice_in_dim(kv_cache, fresh_kv, first_row, 0)
        key_rows = kv_cache[:, :, :head_dim]
        value_rows = kv_cache[:, :, head_dim:]
        scores = jnp.einsum(
            "chd,phd->hcp", query_rows, key_rows, preferred_element_type=jnp.float32
        ) / jnp.sqrt(jnp.float32(head_dim))
        same_req = row_req[:, None] == seq_req[None, :]
        scores = jnp.where(same_req[None], scores, -jnp.inf)
        row_top = jnp.max(scores, axis=-1, keepdims=True)
        weights = jnp.exp(scores - row_top)
        weight_sum = jnp.sum(weights, axis=-1, keepdims=True)
        attention = (weights / weight_sum).astype(jnp.bfloat16)
        attended = jnp.einsum(
            "hcp,phd->chd", attention, value_rows, preferred_element_type=jnp.float32
        ).astype(jnp.bfloat16)
        attended = attended.reshape(span_rows, heads_dev * head_dim)
        mlp_act = gelu_tanh(jnp.dot(normed, mlp_weight, preferred_element_type=jnp.float32)).astype(
            jnp.bfloat16
        )
        partial_value = jnp.dot(attended, attn_out_weight, preferred_element_type=jnp.float32)
        partial_value = partial_value + jnp.dot(
            mlp_act, mlp_out_weight, preferred_element_type=jnp.float32
        )
        branch = lax.psum_scatter(
            partial_value.astype(jnp.bfloat16), "req", scatter_dimension=1, tiled=True
        ).astype(jnp.float32)
        gate_cols = lax.dynamic_slice_in_dim(mod_rows[:, 2], req_index * col_width, col_width, 1)
        updated = (incoming.astype(jnp.float32) + gate_cols * branch).astype(jnp.bfloat16)
        return (updated, kv_cache)

    def advance(moment, carry):
        incoming, kv_cache, results = carry
        span_slot = moment - section_index
        active = (span_slot >= 0) & (span_slot < span_count)
        span_id = span_order[jnp.clip(span_slot, 0, span_count - 1)]
        first_row = span_id * span_rows
        entering = lax.dynamic_slice_in_dim(sequence, first_row, span_rows, 0)
        source = jnp.where(section_index == 0, entering, incoming)
        computed, new_cache = work(source, kv_cache, span_id)
        updated = jnp.where(active, computed, jnp.zeros_like(computed))
        kv_cache = jnp.where(active, new_cache, kv_cache)
        store_here = active & (section_index == section_count - 1)
        current = lax.dynamic_slice_in_dim(results, first_row, span_rows, 0)
        results = lax.dynamic_update_slice_in_dim(
            results, jnp.where(store_here, updated, current), first_row, 0
        )
        incoming = from_behind(updated, "section", 1)
        return (incoming, kv_cache, results)

    start_state = (
        jnp.zeros((span_rows, in_width), jnp.bfloat16),
        stale_kv[0],
        jnp.zeros((patches, in_width), jnp.bfloat16),
    )
    last_in, last_cache, results = lax.fori_loop(
        0, span_count + section_count - 1, advance, start_state
    )
    finished = spread_2(results, "section", section_count - 1)
    inverse = jnp.zeros((patches,), jnp.int32).at[patch_route].set(patch_ids)
    unrouted = finished[inverse]
    owned = lax.all_to_all(unrouted, "req", split_axis=0, concat_axis=1, tiled=True)
    return lax.dynamic_slice_in_dim(owned, section_index * section_cols, section_cols, 1)


def solution(mesh):
    in_specs = (
        P("req", None),
        P(),
        P(),
        P(),
        P("section", None, None, None),
        P("section", None, "req", None),
        P("section", None, "req"),
        P("section", "req", None, None),
        P("section", "req", None),
        P("section", None, "req", None),
    )
    out_specs = P("req", "section")
    return jax.shard_map(shards, mesh=mesh, in_specs=in_specs, out_specs=out_specs, check_vma=False)
```

profile of v0, /device:TPU:1, one launch (start us, length us, event | category | flops | bytes accessed | tf_op | source)
XLA Modules:
  0.0 2296.1 jit_solution(89671729935915630)
XLA Ops:
  8.2 7.6 all-to-all-start
  23.9 2208.2 %while.20 = (s32[]{:T(128)}, bf16[64,192]{1,0:T(8,128)(2,1)S(1)}, bf16[128,1,256]{2,0,1:T(8,128)(2,1)S(1)}, bf16[128,192]{1,0:T(8,128)(2,1)S(1)}, s32[]{:T(128)}...) while((s32[]{:T(128)}, bf16[64,192]{1,0:T(8,128)(2,1)S(1)}, ...), condition=%wide.region_8.9_spmd.clone, body=%wide.region_2.8_spmd.clone.sunk | while | flops 623784896 | bytes 52648204 | solution.py:142
  25.3 18.8 all-gather.3
  66.4 81.7 %reduce-scatter.6.cloned.1.call-done = bf16[192,64]{1,0:T(8,128)(2,1)} async-done(((bf16[3072,64]{1,0:T(8,128)(2,1)}), bf16[192,64]{1,0:T(8,128)(2,1)}) %reduce-scatter.6.cloned.1.call-update) | async-done | bytes 24592 | tf_op jit(solution)/shard_map/while
  149.0 5.3 collective-permute-start
  156.8 17.8 all-gather.3
  190.2 3.6 fusion.79
  196.8 81.1 %reduce-scatter.6.cloned.1.call-done = bf16[192,64]{1,0:T(8,128)(2,1)} async-done(((bf16[3072,64]{1,0:T(8,128)(2,1)}), bf16[192,64]{1,0:T(8,128)(2,1)}) %reduce-scatter.6.cloned.1.call-update) | async-done | bytes 24592 | tf_op jit(solution)/shard_map/while
  278.8 5.3 collective-permute-start
  286.6 17.8 all-gather.3
  320.0 3.6 fusion.79
  326.6 81.1 %reduce-scatter.6.cloned.1.call-done = bf16[192,64]{1,0:T(8,128)(2,1)} async-done(((bf16[3072,64]{1,0:T(8,128)(2,1)}), bf16[192,64]{1,0:T(8,128)(2,1)}) %reduce-scatter.6.cloned.1.call-update) | async-done | bytes 24592 | tf_op jit(solution)/shard_map/while
  408.6 5.4 collective-permute-start
  416.3 17.8 all-gather.3
  456.3 81.1 %reduce-scatter.6.cloned.1.call-done = bf16[192,64]{1,0:T(8,128)(2,1)} async-done(((bf16[3072,64]{1,0:T(8,128)(2,1)}), bf16[192,64]{1,0:T(8,128)(2,1)}) %reduce-scatter.6.cloned.1.call-update) | async-done | bytes 24592 | tf_op jit(solution)/shard_map/while
  538.4 5.3 collective-permute-start
  546.1 17.8 all-gather.3
  586.1 81.1 %reduce-scatter.6.cloned.1.call-done = bf16[192,64]{1,0:T(8,128)(2,1)} async-done(((bf16[3072,64]{1,0:T(8,128)(2,1)}), bf16[192,64]{1,0:T(8,128)(2,1)}) %reduce-scatter.6.cloned.1.call-update) | async-done | bytes 24592 | tf_op jit(solution)/shard_map/while
  668.2 5.3 collective-permute-start
  675.9 17.8 all-gather.3
  715.9 81.1 %reduce-scatter.6.cloned.1.call-done = bf16[192,64]{1,0:T(8,128)(2,1)} async-done(((bf16[3072,64]{1,0:T(8,128)(2,1)}), bf16[192,64]{1,0:T(8,128)(2,1)}) %reduce-scatter.6.cloned.1.call-update) | async-done | bytes 24592 | tf_op jit(solution)/shard_map/while
  797.9 5.3 collective-permute-start
  805.7 17.8 all-gather.3
  839.1 3.6 fusion.79
  845.7 81.1 %reduce-scatter.6.cloned.1.call-done = bf16[192,64]{1,0:T(8,128)(2,1)} async-done(((bf16[3072,64]{1,0:T(8,128)(2,1)}), bf16[192,64]{1,0:T(8,128)(2,1)}) %reduce-scatter.6.cloned.1.call-update) | async-done | bytes 24592 | tf_op jit(solution)/shard_map/while
  927.7 5.3 collective-permute-start
  935.5 17.8 all-gather.3
  975.5 81.0 %reduce-scatter.6.cloned.1.call-done = bf16[192,64]{1,0:T(8,128)(2,1)} async-done(((bf16[3072,64]{1,0:T(8,128)(2,1)}), bf16[192,64]{1,0:T(8,128)(2,1)}) %reduce-scatter.6.cloned.1.call-update) | async-done | bytes 24592 | tf_op jit(solution)/shard_map/while
  1057.5 5.4 collective-permute-start
  1065.3 17.8 all-gather.3
  1098.7 3.6 fusion.79
  1105.3 81.1 %reduce-scatter.6.cloned.1.call-done = bf16[192,64]{1,0:T(8,128)(2,1)} async-done(((bf16[3072,64]{1,0:T(8,128)(2,1)}), bf16[192,64]{1,0:T(8,128)(2,1)}) %reduce-scatter.6.cloned.1.call-update) | async-done | bytes 24592 | tf_op jit(solution)/shard_map/while
  1187.3 5.3 collective-permute-start
  1195.0 17.8 all-gather.3
  1228.4 3.6 fusion.79
  1235.0 81.2 %reduce-scatter.6.cloned.1.call-done = bf16[192,64]{1,0:T(8,128)(2,1)} async-done(((bf16[3072,64]{1,0:T(8,128)(2,1)}), bf16[192,64]{1,0:T(8,128)(2,1)}) %reduce-scatter.6.cloned.1.call-update) | async-done | bytes 24592 | tf_op jit(solution)/shard_map/while
  1317.2 5.4 collective-permute-start
  1325.0 17.8 all-gather.3
  1365.0 81.1 %reduce-scatter.6.cloned.1.call-done = bf16[192,64]{1,0:T(8,128)(2,1)} async-done(((bf16[3072,64]{1,0:T(8,128)(2,1)}), bf16[192,64]{1,0:T(8,128)(2,1)}) %reduce-scatter.6.cloned.1.call-update) | async-done | bytes 24592 | tf_op jit(solution)/shard_map/while
  1447.0 5.3 collective-permute-start
  1454.7 17.8 all-gather.3
  1494.8 81.1 %reduce-scatter.6.cloned.1.call-done = bf16[192,64]{1,0:T(8,128)(2,1)} async-done(((bf16[3072,64]{1,0:T(8,128)(2,1)}), bf16[192,64]{1,0:T(8,128)(2,1)}) %reduce-scatter.6.cloned.1.call-update) | async-done | bytes 24592 | tf_op jit(solution)/shard_map/while
  1576.8 5.3 collective-permute-start
  1584.6 17.8 all-gather.3
  1618.0 3.6 fusion.79
  1624.6 81.1 %reduce-scatter.6.cloned.1.call-done = bf16[192,64]{1,0:T(8,128)(2,1)} async-done(((bf16[3072,64]{1,0:T(8,128)(2,1)}), bf16[192,64]{1,0:T(8,128)(2,1)}) %reduce-scatter.6.cloned.1.call-update) | async-done | bytes 24592 | tf_op jit(solution)/shard_map/while
  1706.6 5.4 collective-permute-start
  1714.4 17.8 all-gather.3
  1754.4 81.1 %reduce-scatter.6.cloned.1.call-done = bf16[192,64]{1,0:T(8,128)(2,1)} async-done(((bf16[3072,64]{1,0:T(8,128)(2,1)}), bf16[192,64]{1,0:T(8,128)(2,1)}) %reduce-scatter.6.cloned.1.call-update) | async-done | bytes 24592 | tf_op jit(solution)/shard_map/while
  1836.4 5.4 collective-permute-start
  1844.2 17.8 all-gather.3
  1884.2 81.1 %reduce-scatter.6.cloned.1.call-done = bf16[192,64]{1,0:T(8,128)(2,1)} async-done(((bf16[3072,64]{1,0:T(8,128)(2,1)}), bf16[192,64]{1,0:T(8,128)(2,1)}) %reduce-scatter.6.cloned.1.call-update) | async-done | bytes 24592 | tf_op jit(solution)/shard_map/while
  1966.2 5.3 collective-permute-start
  1973.9 17.7 all-gather.3
  2007.3 3.6 fusion.79
  2013.9 81.1 %reduce-scatter.6.cloned.1.call-done = bf16[192,64]{1,0:T(8,128)(2,1)} async-done(((bf16[3072,64]{1,0:T(8,128)(2,1)}), bf16[192,64]{1,0:T(8,128)(2,1)}) %reduce-scatter.6.cloned.1.call-update) | async-done | bytes 24592 | tf_op jit(solution)/shard_map/while
  2095.9 5.3 collective-permute-start
  2103.7 17.8 all-gather.3
  2137.1 3.6 fusion.79
  2143.7 81.0 %reduce-scatter.6.cloned.1.call-done = bf16[192,64]{1,0:T(8,128)(2,1)} async-done(((bf16[3072,64]{1,0:T(8,128)(2,1)}), bf16[192,64]{1,0:T(8,128)(2,1)}) %reduce-scatter.6.cloned.1.call-update) | async-done | bytes 24592 | tf_op jit(solution)/shard_map/while
  2225.7 5.3 collective-permute-start
  2232.1 44.1 %psum.7 = bf16[128,192]{1,0:T(8,128)(2,1)S(1)} all-reduce(bf16[128,192]{1,0:T(8,128)(2,1)S(1)} %broadcast_select_fusion.1), channel_id=1, replica_groups=mesh['section'=16,'req'=16] {'section'}, use_global_device_ids=true, to_apply=%region_9.10 | all-reduce | flops 24576 | bytes 98304 | tf_op jit(solution)/shard_map/psum | solution.py:15
  2277.6 4.6 all-to-all-start.1
  2282.3 6.5 all-to-all-done.1
  (634 shorter events, 402.8 us)
Async XLA Ops:
  6.5 17.3 copy-start.5
  6.5 17.3 copy-start.4
  8.2 14.8 all-to-all-start
  23.9 124.2 %reduce-scatter.6.cloned.1.call-start = ((), (), s32[]{:S(2)}) async-start(), calls=%async_computation.3 | async-start | bytes 835584 | tf_op jit(solution)/shard_map/while
  55.6 2.0 copy-start.1
  59.8 3.8 copy-start.3
  149.0 6.3 collective-permute-start
  155.4 122.5 %reduce-scatter.6.cloned.1.call-start = ((), (), s32[]{:S(2)}) async-start(), calls=%async_computation.3 | async-start | bytes 835584 | tf_op jit(solution)/shard_map/while
  186.0 2.0 copy-start.1
  190.2 3.8 copy-start.3
  278.8 6.4 collective-permute-start
  285.2 122.5 %reduce-scatter.6.cloned.1.call-start = ((), (), s32[]{:S(2)}) async-start(), calls=%async_computation.3 | async-start | bytes 835584 | tf_op jit(solution)/shard_map/while
  315.8 2.0 copy-start.1
  320.0 3.8 copy-start.3
  408.6 6.4 collective-permute-start
  414.9 122.5 %reduce-scatter.6.cloned.1.call-start = ((), (), s32[]{:S(2)}) async-start(), calls=%async_computation.3 | async-start | bytes 835584 | tf_op jit(solution)/shard_map/while
  445.6 2.0 copy-start.1
  449.7 3.8 copy-start.3
  538.4 6.3 collective-permute-start
  544.7 122.5 %reduce-scatter.6.cloned.1.call-start = ((), (), s32[]{:S(2)}) async-start(), calls=%async_computation.3 | async-start | bytes 835584 | tf_op jit(solution)/shard_map/while
  575.4 2.0 copy-start.1
  579.5 3.8 copy-start.3
  668.2 6.4 collective-permute-start
  674.5 122.5 %reduce-scatter.6.cloned.1.call-start = ((), (), s32[]{:S(2)}) async-start(), calls=%async_computation.3 | async-start | bytes 835584 | tf_op jit(solution)/shard_map/while
  705.2 2.0 copy-start.1
  709.3 3.8 copy-start.3
  797.9 6.4 collective-permute-start
  804.3 122.5 %reduce-scatter.6.cloned.1.call-start = ((), (), s32[]{:S(2)}) async-start(), calls=%async_computation.3 | async-start | bytes 835584 | tf_op jit(solution)/shard_map/while
  839.1 3.8 copy-start.3
  927.7 6.3 collective-permute-start
  934.1 122.5 %reduce-scatter.6.cloned.1.call-start = ((), (), s32[]{:S(2)}) async-start(), calls=%async_computation.3 | async-start | bytes 835584 | tf_op jit(solution)/shard_map/while
  964.7 2.0 copy-start.1
  968.9 3.8 copy-start.3
  1057.5 6.4 collective-permute-start
  1063.9 122.5 %reduce-scatter.6.cloned.1.call-start = ((), (), s32[]{:S(2)}) async-start(), calls=%async_computation.3 | async-start | bytes 835584 | tf_op jit(solution)/shard_map/while
  1098.6 3.8 copy-start.3
  1187.3 6.3 collective-permute-start
  1193.6 122.7 %reduce-scatter.6.cloned.1.call-start = ((), (), s32[]{:S(2)}) async-start(), calls=%async_computation.3 | async-start | bytes 835584 | tf_op jit(solution)/shard_map/while
  1228.4 3.8 copy-start.3
  1317.2 6.4 collective-permute-start
  1323.6 122.5 %reduce-scatter.6.cloned.1.call-start = ((), (), s32[]{:S(2)}) async-start(), calls=%async_computation.3 | async-start | bytes 835584 | tf_op jit(solution)/shard_map/while
  1354.2 2.0 copy-start.1
  1358.4 3.8 copy-start.3
  1447.0 6.3 collective-permute-start
  1453.3 122.6 %reduce-scatter.6.cloned.1.call-start = ((), (), s32[]{:S(2)}) async-start(), calls=%async_computation.3 | async-start | bytes 835584 | tf_op jit(solution)/shard_map/while
  1488.1 3.8 copy-start.3
  1576.8 6.4 collective-permute-start
  1583.2 122.5 %reduce-scatter.6.cloned.1.call-start = ((), (), s32[]{:S(2)}) async-start(), calls=%async_computation.3 | async-start | bytes 835584 | tf_op jit(solution)/shard_map/while
  1613.8 2.0 copy-start.1
  1618.0 3.8 copy-start.3
  1706.6 6.4 collective-permute-start
  1713.0 122.5 %reduce-scatter.6.cloned.1.call-start = ((), (), s32[]{:S(2)}) async-start(), calls=%async_computation.3 | async-start | bytes 835584 | tf_op jit(solution)/shard_map/while
  1747.8 3.8 copy-start.3
  1836.4 6.4 collective-permute-start
  1842.8 122.5 %reduce-scatter.6.cloned.1.call-start = ((), (), s32[]{:S(2)}) async-start(), calls=%async_computation.3 | async-start | bytes 835584 | tf_op jit(solution)/shard_map/while
  1877.6 3.8 copy-start.3
  1966.2 6.4 collective-permute-start
  1972.6 122.5 %reduce-scatter.6.cloned.1.call-start = ((), (), s32[]{:S(2)}) async-start(), calls=%async_computation.3 | async-start | bytes 835584 | tf_op jit(solution)/shard_map/while
  2007.3 3.8 copy-start.3
  2095.9 6.3 collective-permute-start
  2102.3 122.5 %reduce-scatter.6.cloned.1.call-start = ((), (), s32[]{:S(2)}) async-start(), calls=%async_computation.3 | async-start | bytes 835584 | tf_op jit(solution)/shard_map/while
  2137.1 3.8 copy-start.3
  2225.7 6.4 collective-permute-start
  2277.6 11.2 all-to-all-start.1
  (42 other events, 79.4 us)
Sparse Core Ops, SparseCore 0:
  65.4 82.6 reduce-scatter.5
  195.8 82.0 reduce-scatter.5
  325.6 82.0 reduce-scatter.5
  455.3 82.0 reduce-scatter.5
  585.1 82.0 reduce-scatter.5
  714.9 82.0 reduce-scatter.5
  844.7 82.0 reduce-scatter.5
  974.5 81.9 reduce-scatter.5
  1104.3 82.0 reduce-scatter.5
  1234.0 82.1 reduce-scatter.5
  1364.0 82.0 reduce-scatter.5
  1493.8 82.0 reduce-scatter.5
  1623.6 82.0 reduce-scatter.5
  1753.4 82.0 reduce-scatter.5
  1883.2 82.0 reduce-scatter.5
  2012.9 82.0 reduce-scatter.5
  2142.7 81.9 reduce-scatter.5
where the time goes:
time: 2300 us
  waiting for transfers between devices  1400 us (61%)
  blocking collectives  348 us (15%)
  local copies, waits for them, and re-layouts  252 us (11%)
  matrix products  143 us (6%)
  starting transfers between devices  103 us (4%)
    while x34, waiting for transfers between devices  1380 us
    all_gather x17, blocking collectives, work(): current = lax.all_gather(incoming, 'req', axis=1, tiled=True)  303 us
    ppermute x17, starting transfers between devices, from_behind(): return lax.ppermute(block, axis, route)  90.9 us
    dot_general x17, matrix products, work(): jnp.dot(mlp_act, mlp_out_weight, preferred_element_type=jnp.float32)  61.6 us
    dot_general x17, matrix products, work(): jnp.dot(onehot, mod_table, precision=lax.Precision.HIGHEST)  61.2 us
    reshape x17, local copies, waits for them, and re-layouts, work(): jnp.dot(onehot, mod_table, precision=lax.Precision.HIGHEST)  59.2 us
    while x187, local copies, waits for them, and re-layouts  51.9 us
    convert_element_type x34, local copies, waits for them, and re-layouts, work(): current.astype(jnp.float32)  51.3 us
  transfers between devices with their start and end apart: 36, of which 35 were waited for; matrix products, arithmetic and copies ran while one was open for 1% of the time, Pallas kernels for 0%

commit v1 on v0

v1 whole, which is shorter than its diff:
```python
import jax
import jax.numpy as jnp
from jax import lax
from jax.sharding import PartitionSpec as P

AXES = ("section", "req")
BF16 = jnp.bfloat16


def gelu_tanh(values):
    return (
        0.5
        * values
        * (1.0 + jnp.tanh(0.7978845608028654 * (values + 0.044715 * values * values * values)))
    )


def layer_norm(values):
    row_mean = jnp.mean(values, axis=-1, keepdims=True)
    centered = values - row_mean
    row_var = jnp.mean(centered * centered, axis=-1, keepdims=True)
    return centered * lax.rsqrt(row_var + 1e-06)


def shards(
    latents,
    patch_route,
    request_len,
    span_order,
    modulation,
    w_qkv,
    w_mlp_in,
    w_out_attn,
    w_out_mlp,
    stale_kv,
):
    section_count = lax.axis_size("section")
    req_count = lax.axis_size("req")
    section_index = lax.axis_index("section")
    req_index = lax.axis_index("req")
    patches = patch_route.shape[0]
    span_rows = patches // span_order.shape[0]
    own_rows, width = latents.shape
    req_total = request_len.shape[0]
    head_dim = w_qkv.shape[3] // 3

    starts = jnp.cumsum(request_len) - request_len
    rows = jnp.arange(patches, dtype=jnp.int32)
    row_req = jnp.sum((rows[:, None] >= starts[None, :]).astype(jnp.int32), axis=1) - 1
    at_position = rows[:, None] == patch_route[None, :]
    positions = jnp.sum(jnp.where(at_position, rows[None, :], 0), axis=1)
    is_first = positions // span_rows == span_order[0]
    same_req = row_req[:, None] == row_req[None, :]
    from_stale = is_first[:, None] & ~is_first[None, :]
    stale = jnp.dot(
        at_position.astype(BF16), stale_kv[0, :, 0], preferred_element_type=jnp.float32
    ).astype(BF16)
    owned_req = lax.dynamic_slice_in_dim(row_req, req_index * own_rows, own_rows, 0)
    onehot = (owned_req[:, None] == jnp.arange(req_total, dtype=jnp.int32)[None, :]).astype(
        jnp.float32
    )
    mod = jnp.einsum("cr,rkd->kcd", onehot, modulation[0], precision=lax.Precision.HIGHEST)

    qkv_weight, mlp_weight = w_qkv[0, :, 0], w_mlp_in[0]
    attn_out_weight, mlp_out_weight = w_out_attn[0, 0], w_out_mlp[0]

    def heads_and_units(normed):
        qkv_rows = jnp.dot(normed, qkv_weight, preferred_element_type=jnp.float32).astype(BF16)
        query, key, value = (
            qkv_rows[:, :head_dim],
            qkv_rows[:, head_dim : 2 * head_dim],
            qkv_rows[:, 2 * head_dim :],
        )
        against_fresh = jnp.dot(query, key.T, preferred_element_type=jnp.float32)
        against_stale = jnp.dot(query, stale[:, :head_dim].T, preferred_element_type=jnp.float32)
        scores = jnp.where(from_stale, against_stale, against_fresh) / jnp.sqrt(
            jnp.float32(head_dim)
        )
        scores = jnp.where(same_req, scores, -jnp.inf)
        row_top = jnp.max(scores, axis=-1, keepdims=True)
        exps = jnp.exp(scores - row_top)
        attention = (exps / jnp.sum(exps, axis=-1, keepdims=True)).astype(BF16)
        none = jnp.zeros_like(attention)
        attended = jnp.dot(
            jnp.where(from_stale, none, attention), value, preferred_element_type=jnp.float32
        ) + jnp.dot(
            jnp.where(from_stale, attention, none),
            stale[:, head_dim:],
            preferred_element_type=jnp.float32,
        )
        mlp_act = gelu_tanh(
            jnp.dot(normed, mlp_weight, preferred_element_type=jnp.float32)
        ).astype(BF16)
        partial_value = jnp.dot(
            attended.astype(BF16), attn_out_weight, preferred_element_type=jnp.float32
        ) + jnp.dot(mlp_act, mlp_out_weight, preferred_element_type=jnp.float32)
        return partial_value.astype(BF16)

    def exchange(value):
        return lax.all_to_all(value, "req", split_axis=0, concat_axis=0, tiled=True)

    def section_step(current):
        normed = (layer_norm(current.astype(jnp.float32)) * (1.0 + mod[1]) + mod[0]).astype(BF16)
        everyone = exchange(jnp.broadcast_to(normed[None], (req_count, own_rows, width)))
        partial_value = heads_and_units(everyone.reshape(patches, width))
        shares = exchange(partial_value.reshape(req_count, own_rows, width))
        branch = jnp.sum(shares.astype(jnp.float32), axis=0)
        return (current.astype(jnp.float32) + mod[2] * branch).astype(BF16)

    onward = [(i, i + req_count) for i in range((section_count - 1) * req_count)]

    def advance(turn, current):
        current = lax.cond(section_index == turn, section_step, lambda values: values, current)
        arrived = lax.ppermute(current, AXES, onward)
        return jnp.where(section_index == turn + 1, arrived, current)

    current = lax.fori_loop(0, section_count, advance, latents)
    pieces = current.reshape(own_rows, section_count, width // section_count).swapaxes(0, 1)
    pieces = lax.all_to_all(pieces, "section", split_axis=0, concat_axis=0, tiled=True)
    return pieces[section_count - 1]


def solution(mesh):
    in_specs = (
        P("req", None),
        P(),
        P(),
        P(),
        P("section", None, None, None),
        P("section", None, "req", None),
        P("section", None, "req"),
        P("section", "req", None, None),
        P("section", "req", None),
        P("section", None, "req", None),
    )
    out_specs = P("req", "section")
    return jax.shard_map(shards, mesh=mesh, in_specs=in_specs, out_specs=out_specs, check_vma=False)
```

time: 2300 us -> 665 us (0.29)
  waiting for transfers between devices: 1400 us -> 57.5 us
  local copies, waits for them, and re-layouts: 252 us -> 2.5 us
  starting transfers between devices: 103 us -> 303 us
  matrix products: 143 us -> 8.63 us
  blocking collectives: 348 us -> 288 us
    while x34 -> x0, waiting for transfers between devices: 1380 us -> none
    all_gather x17 -> x0, blocking collectives: 303 us -> none  [work(): current = lax.all_gather(incoming, 'req', axis=1, tiled=True)]
    all_to_all x0 -> x3, blocking collectives: none -> 288 us  [the longest x1 261 us: shards(): lax.all_to_all(pieces, 'section', split_axis=0, concat_axis=0, tiled=True)]
    ppermute x17 -> x16, starting transfers between devices: 90.9 us -> 303 us  [advance(): arrived = lax.ppermute(current, AXES, onward)]
    dot_general x85 -> x8, matrix products: 143 us -> 8.63 us  [the longest x1 4.4 us: heads_and_units(): jnp.dot(mlp_act, mlp_out_weight, preferred_element_type=jnp.float32)]
    reshape x17 -> x1, local copies, waits for them, and re-layouts: 59.2 us -> 0.13 us  [shards(): current.reshape(own_rows, section_count, width // section_count)]
    while x187 -> x0, local copies, waits for them, and re-layouts: 51.9 us -> none
    convert_element_type x34 -> x0, local copies, waits for them, and re-layouts: 51.3 us -> none  [work(): current.astype(jnp.float32)]
  transfers between devices with their start and end apart: 36 -> 16, of which waited for: 35 -> 16; matrix products, arithmetic and copies ran while one was open for 1% -> 0% of each run, Pallas kernels for 0% -> 0%
where the time goes in v1:
time: 665 us; the launch traced here: 664 us
  starting transfers between devices  303 us (46%)
  blocking collectives  288 us (43%)
  waiting for transfers between devices  57.5 us (9%)
  matrix products  8.63 us (1%)
    ppermute x16, starting transfers between devices, advance(): arrived = lax.ppermute(current, AXES, onward)  303 us
    all_to_all x1, blocking collectives, shards(): lax.all_to_all(pieces, 'section', split_axis=0, concat_axis=0, tiled=True)  261 us
    ppermute x16, waiting for transfers between devices, advance(): arrived = lax.ppermute(current, AXES, onward)  57.5 us
    all_to_all x2, blocking collectives, exchange(): return lax.all_to_all(value, 'req', split_axis=0, concat_axis=0, tiled=True)  27.1 us
  transfers between devices with their start and end apart: 16, of which 16 were waited for; matrix products, arithmetic and copies ran while one was open for 0% of the time, Pallas kernels for 0%

profile of v1, /device:TPU:1, one launch (start us, length us, event | category | flops | bytes accessed | tf_op | source)
XLA Modules:
  0.0 664.0 jit_solution(5744020833726928648)
XLA Ops:
  0.0 0.0 copy-start
  0.0 0.9 copy.28
  0.9 0.7 copy.16
  1.6 0.1 reduce
  1.8 0.7 sub.29
  2.4 0.1 convert_reduce_fusion.2
  2.5 0.8 select_reduce_fusion
  3.3 1.0 convolution_convert_fusion.1
  4.3 0.1 dynamic_slice.3
  4.4 0.0 copy-done
  4.4 0.3 convolution_bitcast_fusion
  4.7 0.7 fusion.66
  5.4 397.1 %while.17 = (s32[]{:T(128)}, bf16[8,3072]{1,0:T(8,128)(2,1)S(1)}, s32[]{:T(128)}, f32[3,8,3072]{2,1,0:T(8,128)S(1)}, bf16[3072,384]{1,0:T(8,128)(2,1)}, /*index=...) while((s32[]{:T(128)}, bf16[8,3072]{1,0:T(8,128)(2,1)S(1)}, ...), condition=%wide.region_11.12_spmd.clone, body=%wide.region_3.11_spmd.clone.sunk | while | flops 1026219776 | bytes 29532248 | solution.py:117
  5.4 4.9 collective-permute-start
  10.4 40.2 %collective-permute-done = bf16[8,3072]{1,0:T(8,128)(2,1)S(1)} collective-permute-done((bf16[8,3072]{1,0:T(8,128)(2,1)S(1)}, bf16[8,3072]{1,0:T(8,128)(2,1)S(1)}, u32[]{:S(2)}, u32[]{:S(2)}) %collective-permute-start) | collective-permute-done | bytes 49184 | tf_op jit(solution)/shard_map/while/body/eval_jaxpr/ppermute | solution.py:114
  50.6 35.2 %conditional.3 = (bf16[8,3072]{1,0:T(8,128)(2,1)S(1)}) conditional(s32[]{:T(128)} %convert_element_type.87, bf16[8,3072]{1,0:T(8,128)(2,1)S(1)} %get-tuple-element.378, (bf16[8,3072]{1,0:T(8,128)(2,1)S(1)}, f32[3,8,3072]{2,1,0:T(8,128)S(1)}, bf16[3072,384]{1,0:T(8,128)(2,1)}, bf16[128,256]{1,0:T(8,128)(2,1)S(1)}, pred[128]{0:T(512)(128)(4,1)S(1)}, ...), branch_computations={%region_4.4_spmd, %region_5.10_spmd} | conditional | flops 1026195200 | bytes 29187908 | solution.py:113
  50.6 0.0 copy-start.1
  50.6 0.1 convert_reduce_fusion.1
  50.8 0.2 fusion.24
  51.0 0.1 fusion.27
  51.1 0.1 broadcast_in_dim.13
  51.2 13.2 %all_to_all.13 = bf16[16,8,3072]{2,1,0:T(8,128)(2,1)S(1)} all-to-all(bf16[16,8,3072]{2,1,0:T(8,128)(2,1)S(1)} %broadcast_in_dim.13), channel_id=1, replica_groups=mesh['section'=16,'req'=16] {'req'}, dimensions={0} | all-to-all | bytes 1572864 | tf_op jit(solution)/shard_map/while/body/eval_jaxpr/cond/branch_1_fun/all_to_all | solution.py:100
  64.3 0.0 copy-done.1
  64.3 0.6 convolution_convert_fusion
  64.9 0.1 fusion.39
  65.0 0.2 fusion.68
  65.3 0.3 fusion.34
  65.6 1.7 fusion.9
  67.3 4.4 fusion.5
  71.7 14.0 %all_to_all.14 = bf16[16,8,3072]{2,1,0:T(8,128)(2,1)S(1)} all-to-all(bf16[16,8,3072]{2,1,0:T(8,128)(2,1)} %fusion.5), channel_id=1, replica_groups=mesh['section'=16,'req'=16] {'req'}, dimensions={0} | all-to-all | bytes 1572864 | tf_op jit(solution)/shard_map/while/body/eval_jaxpr/cond/branch_1_fun/all_to_all | solution.py:100
  85.6 0.1 convert_reduce_fusion
  85.8 1.9 collective-permute-start
  87.7 1.2 collective-permute-done
  89.0 41.9 %collective-permute-start = (bf16[8,3072]{1,0:T(8,128)(2,1)S(1)}, bf16[8,3072]{1,0:T(8,128)(2,1)S(1)}, u32[]{:S(2)}, u32[]{:S(2)}) collective-permute-start(bf16[8,3072]{1,0:T(8,128)(2,1)S(1)} %get-tuple-element.403), channel_id=1, source_target_pairs={{0,16},{1,17},{2,18},{3,19},{4,20},{5,21},{6,22},{7,23},{8,24},{9,... | collective-permute-start | bytes 147464 | tf_op jit(solution)/shard_map/while/body/eval_jaxpr/ppermute | solution.py:114
  130.9 1.1 collective-permute-done
  132.1 4.2 collective-permute-start
  136.4 1.1 collective-permute-done
  137.6 34.5 %collective-permute-start = (bf16[8,3072]{1,0:T(8,128)(2,1)S(1)}, bf16[8,3072]{1,0:T(8,128)(2,1)S(1)}, u32[]{:S(2)}, u32[]{:S(2)}) collective-permute-start(bf16[8,3072]{1,0:T(8,128)(2,1)S(1)} %get-tuple-element.403), channel_id=1, source_target_pairs={{0,16},{1,17},{2,18},{3,19},{4,20},{5,21},{6,22},{7,23},{8,24},{9,... | collective-permute-start | bytes 147464 | tf_op jit(solution)/shard_map/while/body/eval_jaxpr/ppermute | solution.py:114
  172.1 1.1 collective-permute-done
  173.3 4.2 collective-permute-start
  177.6 1.1 collective-permute-done
  178.8 39.7 %collective-permute-start = (bf16[8,3072]{1,0:T(8,128)(2,1)S(1)}, bf16[8,3072]{1,0:T(8,128)(2,1)S(1)}, u32[]{:S(2)}, u32[]{:S(2)}) collective-permute-start(bf16[8,3072]{1,0:T(8,128)(2,1)S(1)} %get-tuple-element.403), channel_id=1, source_target_pairs={{0,16},{1,17},{2,18},{3,19},{4,20},{5,21},{6,22},{7,23},{8,24},{9,... | collective-permute-start | bytes 147464 | tf_op jit(solution)/shard_map/while/body/eval_jaxpr/ppermute | solution.py:114
  218.4 1.1 collective-permute-done
  219.6 4.2 collective-permute-start
  223.9 1.1 collective-permute-done
  225.1 34.5 %collective-permute-start = (bf16[8,3072]{1,0:T(8,128)(2,1)S(1)}, bf16[8,3072]{1,0:T(8,128)(2,1)S(1)}, u32[]{:S(2)}, u32[]{:S(2)}) collective-permute-start(bf16[8,3072]{1,0:T(8,128)(2,1)S(1)} %get-tuple-element.403), channel_id=1, source_target_pairs={{0,16},{1,17},{2,18},{3,19},{4,20},{5,21},{6,22},{7,23},{8,24},{9,... | collective-permute-start | bytes 147464 | tf_op jit(solution)/shard_map/while/body/eval_jaxpr/ppermute | solution.py:114
  259.6 1.1 collective-permute-done
  260.8 4.2 collective-permute-start
  265.1 1.1 collective-permute-done
  266.3 39.7 %collective-permute-start = (bf16[8,3072]{1,0:T(8,128)(2,1)S(1)}, bf16[8,3072]{1,0:T(8,128)(2,1)S(1)}, u32[]{:S(2)}, u32[]{:S(2)}) collective-permute-start(bf16[8,3072]{1,0:T(8,128)(2,1)S(1)} %get-tuple-element.403), channel_id=1, source_target_pairs={{0,16},{1,17},{2,18},{3,19},{4,20},{5,21},{6,22},{7,23},{8,24},{9,... | collective-permute-start | bytes 147464 | tf_op jit(solution)/shard_map/while/body/eval_jaxpr/ppermute | solution.py:114
  305.9 1.1 collective-permute-done
  307.1 4.2 collective-permute-start
  311.4 1.1 collective-permute-done
  312.6 34.5 %collective-permute-start = (bf16[8,3072]{1,0:T(8,128)(2,1)S(1)}, bf16[8,3072]{1,0:T(8,128)(2,1)S(1)}, u32[]{:S(2)}, u32[]{:S(2)}) collective-permute-start(bf16[8,3072]{1,0:T(8,128)(2,1)S(1)} %get-tuple-element.403), channel_id=1, source_target_pairs={{0,16},{1,17},{2,18},{3,19},{4,20},{5,21},{6,22},{7,23},{8,24},{9,... | collective-permute-start | bytes 147464 | tf_op jit(solution)/shard_map/while/body/eval_jaxpr/ppermute | solution.py:114
  347.1 1.1 collective-permute-done
  348.3 4.2 collective-permute-start
  352.6 1.1 collective-permute-done
  353.8 40.9 %collective-permute-start = (bf16[8,3072]{1,0:T(8,128)(2,1)S(1)}, bf16[8,3072]{1,0:T(8,128)(2,1)S(1)}, u32[]{:S(2)}, u32[]{:S(2)}) collective-permute-start(bf16[8,3072]{1,0:T(8,128)(2,1)S(1)} %get-tuple-element.403), channel_id=1, source_target_pairs={{0,16},{1,17},{2,18},{3,19},{4,20},{5,21},{6,22},{7,23},{8,24},{9,... | collective-permute-start | bytes 147464 | tf_op jit(solution)/shard_map/while/body/eval_jaxpr/ppermute | solution.py:114
  394.7 1.1 collective-permute-done
  395.9 5.5 collective-permute-start
  401.3 1.1 collective-permute-done
  402.5 0.1 reshape.101
  402.7 260.7 %all_to_all.15 = bf16[16,8,192]{2,1,0:T(8,128)(2,1)S(1)} all-to-all(bf16[16,8,192]{2,1,0:T(8,128)(2,1)S(1)} %copy.17), channel_id=1, replica_groups=mesh['section'=16,'req'=16] {'section'}, dimensions={0} | all-to-all | bytes 98304 | tf_op jit(solution)/shard_map/all_to_all | solution.py:119
  663.4 0.6 slice_bitcast_fusion
  (38 shorter events, 0.5 us)
Async XLA Ops:
  0.0 4.4 copy-start
  5.4 45.2 %collective-permute-start = (bf16[8,3072]{1,0:T(8,128)(2,1)S(1)}, bf16[8,3072]{1,0:T(8,128)(2,1)S(1)}, u32[]{:S(2)}, u32[]{:S(2)}) collective-permute-start(bf16[8,3072]{1,0:T(8,128)(2,1)S(1)} %get-tuple-element.403), channel_id=1, source_target_pairs={{0,16},{1,17},{2,18},{3,19},{4,20},{5,21},{6,22},{7,23},{8,24},{9,... | collective-permute-start | bytes 147464 | tf_op jit(solution)/shard_map/while/body/eval_jaxpr/ppermute | solution.py:114
  50.6 13.7 %copy-start.1 = (bf16[3072,384]{1,0:T(8,128)(2,1)S(1)}, bf16[3072,384]{1,0:T(8,128)(2,1)}, u32[]{:S(2)}) copy-start(bf16[3072,384]{1,0:T(8,128)(2,1)} %get-tuple-element.206) | copy-start | bytes 7077892 | tf_op jit(solution)/shard_map/while/body/eval_jaxpr/cond
  85.8 3.1 collective-permute-start
  89.0 43.1 %collective-permute-start = (bf16[8,3072]{1,0:T(8,128)(2,1)S(1)}, bf16[8,3072]{1,0:T(8,128)(2,1)S(1)}, u32[]{:S(2)}, u32[]{:S(2)}) collective-permute-start(bf16[8,3072]{1,0:T(8,128)(2,1)S(1)} %get-tuple-element.403), channel_id=1, source_target_pairs={{0,16},{1,17},{2,18},{3,19},{4,20},{5,21},{6,22},{7,23},{8,24},{9,... | collective-permute-start | bytes 147464 | tf_op jit(solution)/shard_map/while/body/eval_jaxpr/ppermute | solution.py:114
  132.1 5.4 collective-permute-start
  137.6 35.7 %collective-permute-start = (bf16[8,3072]{1,0:T(8,128)(2,1)S(1)}, bf16[8,3072]{1,0:T(8,128)(2,1)S(1)}, u32[]{:S(2)}, u32[]{:S(2)}) collective-permute-start(bf16[8,3072]{1,0:T(8,128)(2,1)S(1)} %get-tuple-element.403), channel_id=1, source_target_pairs={{0,16},{1,17},{2,18},{3,19},{4,20},{5,21},{6,22},{7,23},{8,24},{9,... | collective-permute-start | bytes 147464 | tf_op jit(solution)/shard_map/while/body/eval_jaxpr/ppermute | solution.py:114
  173.3 5.4 collective-permute-start
  178.8 40.8 %collective-permute-start = (bf16[8,3072]{1,0:T(8,128)(2,1)S(1)}, bf16[8,3072]{1,0:T(8,128)(2,1)S(1)}, u32[]{:S(2)}, u32[]{:S(2)}) collective-permute-start(bf16[8,3072]{1,0:T(8,128)(2,1)S(1)} %get-tuple-element.403), channel_id=1, source_target_pairs={{0,16},{1,17},{2,18},{3,19},{4,20},{5,21},{6,22},{7,23},{8,24},{9,... | collective-permute-start | bytes 147464 | tf_op jit(solution)/shard_map/while/body/eval_jaxpr/ppermute | solution.py:114
  219.6 5.4 collective-permute-start
  225.1 35.7 %collective-permute-start = (bf16[8,3072]{1,0:T(8,128)(2,1)S(1)}, bf16[8,3072]{1,0:T(8,128)(2,1)S(1)}, u32[]{:S(2)}, u32[]{:S(2)}) collective-permute-start(bf16[8,3072]{1,0:T(8,128)(2,1)S(1)} %get-tuple-element.403), channel_id=1, source_target_pairs={{0,16},{1,17},{2,18},{3,19},{4,20},{5,21},{6,22},{7,23},{8,24},{9,... | collective-permute-start | bytes 147464 | tf_op jit(solution)/shard_map/while/body/eval_jaxpr/ppermute | solution.py:114
  260.8 5.4 collective-permute-start
  266.3 40.8 %collective-permute-start = (bf16[8,3072]{1,0:T(8,128)(2,1)S(1)}, bf16[8,3072]{1,0:T(8,128)(2,1)S(1)}, u32[]{:S(2)}, u32[]{:S(2)}) collective-permute-start(bf16[8,3072]{1,0:T(8,128)(2,1)S(1)} %get-tuple-element.403), channel_id=1, source_target_pairs={{0,16},{1,17},{2,18},{3,19},{4,20},{5,21},{6,22},{7,23},{8,24},{9,... | collective-permute-start | bytes 147464 | tf_op jit(solution)/shard_map/while/body/eval_jaxpr/ppermute | solution.py:114
  307.1 5.4 collective-permute-start
  312.6 35.7 %collective-permute-start = (bf16[8,3072]{1,0:T(8,128)(2,1)S(1)}, bf16[8,3072]{1,0:T(8,128)(2,1)S(1)}, u32[]{:S(2)}, u32[]{:S(2)}) collective-permute-start(bf16[8,3072]{1,0:T(8,128)(2,1)S(1)} %get-tuple-element.403), channel_id=1, source_target_pairs={{0,16},{1,17},{2,18},{3,19},{4,20},{5,21},{6,22},{7,23},{8,24},{9,... | collective-permute-start | bytes 147464 | tf_op jit(solution)/shard_map/while/body/eval_jaxpr/ppermute | solution.py:114
  348.3 5.4 collective-permute-start
  353.8 42.0 %collective-permute-start = (bf16[8,3072]{1,0:T(8,128)(2,1)S(1)}, bf16[8,3072]{1,0:T(8,128)(2,1)S(1)}, u32[]{:S(2)}, u32[]{:S(2)}) collective-permute-start(bf16[8,3072]{1,0:T(8,128)(2,1)S(1)} %get-tuple-element.403), channel_id=1, source_target_pairs={{0,16},{1,17},{2,18},{3,19},{4,20},{5,21},{6,22},{7,23},{8,24},{9,... | collective-permute-start | bytes 147464 | tf_op jit(solution)/shard_map/while/body/eval_jaxpr/ppermute | solution.py:114
  395.9 6.6 collective-permute-start

commit v2 on v1

v2 whole, which is shorter than its diff:
```python
import functools

import jax
import jax.numpy as jnp
from jax import lax
from jax.experimental import pallas as pl
from jax.experimental.pallas import tpu as pltpu
from jax.sharding import PartitionSpec as P

AXES = ("section", "req")
BF16 = jnp.bfloat16
WIDTH_CUTS = 4
TILE = 16
VMEM = pl.BlockSpec(memory_space=pltpu.VMEM)
ANY = pl.BlockSpec(memory_space=pl.ANY)
PARAMS = pltpu.CompilerParams(vmem_limit_bytes=16 * 1024 * 1024)


def gelu_tanh(values):
    return (
        0.5
        * values
        * (1.0 + jnp.tanh(0.7978845608028654 * (values + 0.044715 * values * values * values)))
    )


def block_kernel(
    head_dim,
    rows_ref,
    qkv_ref,
    mlp_ref,
    attn_out_ref,
    mlp_out_ref,
    stale_ref,
    from_stale_ref,
    bias_ref,
    out_ref,
):
    qkv = jnp.dot(rows_ref[...], qkv_ref[...], preferred_element_type=jnp.float32).astype(BF16)
    query, key, value = (
        qkv[:, :head_dim],
        qkv[:, head_dim : 2 * head_dim],
        qkv[:, 2 * head_dim :],
    )
    across = (((1,), (1,)), ((), ()))
    against_fresh = lax.dot_general(query, key, across, preferred_element_type=jnp.float32)
    against_stale = lax.dot_general(
        query, stale_ref[:, :head_dim], across, preferred_element_type=jnp.float32
    )
    from_stale = from_stale_ref[...] > 0.0
    scores = jnp.where(from_stale, against_stale, against_fresh) / jnp.sqrt(
        jnp.float32(head_dim)
    )
    scores = scores + bias_ref[...]
    exps = jnp.exp(scores - jnp.max(scores, axis=-1, keepdims=True))
    attention = exps / jnp.sum(exps, axis=-1, keepdims=True)
    attended = jnp.dot(
        jnp.where(from_stale, 0.0, attention).astype(BF16),
        value,
        preferred_element_type=jnp.float32,
    ) + jnp.dot(
        jnp.where(from_stale, attention, 0.0).astype(BF16),
        stale_ref[:, head_dim:],
        preferred_element_type=jnp.float32,
    )
    attended = attended.astype(BF16)
    mlp_act = gelu_tanh(
        jnp.dot(rows_ref[...], mlp_ref[...], preferred_element_type=jnp.float32)
    ).astype(BF16)
    cols = out_ref.shape[1] // WIDTH_CUTS
    for cut in range(WIDTH_CUTS):
        span = slice(cut * cols, (cut + 1) * cols)
        out_ref[:, span] = (
            jnp.dot(attended, attn_out_ref[:, span], preferred_element_type=jnp.float32)
            + jnp.dot(mlp_act, mlp_out_ref[:, span], preferred_element_type=jnp.float32)
        ).astype(BF16)


def spread_normed(current, mod_ref, out_ref):
    row_mean = jnp.mean(current, axis=-1, keepdims=True)
    centered = current - row_mean
    row_var = jnp.mean(centered * centered, axis=-1, keepdims=True)
    normed = centered * lax.rsqrt(row_var + 1e-06) * (1.0 + mod_ref[1]) + mod_ref[0]
    twice = jnp.concatenate([normed, normed], axis=0).astype(BF16)
    for first in range(0, out_ref.shape[0], TILE):
        out_ref[first : first + TILE, :] = twice


def summed(shares_ref, current_ref, mod_ref):
    branch = shares_ref[:TILE, :].astype(jnp.float32)
    for first in range(TILE, shares_ref.shape[0], TILE):
        branch = branch + shares_ref[first : first + TILE, :].astype(jnp.float32)
    branch = branch[: TILE // 2] + branch[TILE // 2 :]
    return (current_ref[...].astype(jnp.float32) + mod_ref[2] * branch).astype(BF16)


def norm_kernel(current_ref, mod_ref, *refs):
    spread_normed(current_ref[...].astype(jnp.float32), mod_ref, refs[-1])


def sum_kernel(shares_ref, current_ref, mod_ref, out_ref):
    out_ref[...] = summed(shares_ref, current_ref, mod_ref)


def shards(
    latents,
    patch_route,
    request_len,
    span_order,
    modulation,
    w_qkv,
    w_mlp_in,
    w_out_attn,
    w_out_mlp,
    stale_kv,
):
    section_count = lax.axis_size("section")
    req_count = lax.axis_size("req")
    section_index = lax.axis_index("section")
    req_index = lax.axis_index("req")
    patches = patch_route.shape[0]
    span_rows = patches // span_order.shape[0]
    own_rows, width = latents.shape
    req_total = request_len.shape[0]
    head_dim = w_qkv.shape[3] // 3

    starts = jnp.cumsum(request_len) - request_len
    rows = jnp.arange(patches, dtype=jnp.int32)
    row_req = jnp.sum((rows[:, None] >= starts[None, :]).astype(jnp.int32), axis=1) - 1
    at_position = rows[:, None] == patch_route[None, :]
    positions = jnp.sum(jnp.where(at_position, rows[None, :], 0), axis=1)
    is_first = positions // span_rows == span_order[0]
    same_req = row_req[:, None] == row_req[None, :]
    from_stale = (is_first[:, None] & ~is_first[None, :]).astype(jnp.float32)
    bias = jnp.where(same_req, 0.0, -jnp.inf).astype(jnp.float32)
    stale = jnp.dot(
        at_position.astype(BF16), stale_kv[0, :, 0], preferred_element_type=jnp.float32
    ).astype(BF16)
    owned_req = lax.dynamic_slice_in_dim(row_req, req_index * own_rows, own_rows, 0)
    onehot = (owned_req[:, None] == jnp.arange(req_total, dtype=jnp.int32)[None, :]).astype(
        jnp.float32
    )
    mod = jnp.einsum("cr,rkd->kcd", onehot, modulation[0], precision=lax.Precision.HIGHEST)
    held = lax.optimization_barrier((mod, stale, from_stale, bias))
    mod, stale, from_stale, bias = held
    weights = (w_qkv[0, :, 0], w_mlp_in[0], w_out_attn[0, 0], w_out_mlp[0])

    all_rows = jax.ShapeDtypeStruct((patches, width), BF16)
    own = jax.ShapeDtypeStruct((own_rows, width), BF16)
    norm = pl.pallas_call(
        norm_kernel,
        out_shape=all_rows,
        in_specs=[VMEM] * 2 + [ANY] * 4,
        out_specs=VMEM,
        compiler_params=PARAMS,
        name="spread_normed",
    )
    heads_and_units = pl.pallas_call(
        functools.partial(block_kernel, head_dim),
        out_shape=all_rows,
        in_specs=[VMEM] * 8,
        out_specs=VMEM,
        compiler_params=PARAMS,
        name="heads_and_units",
    )
    add_shares = pl.pallas_call(
        sum_kernel,
        out_shape=own,
        in_specs=[VMEM] * 3,
        out_specs=VMEM,
        compiler_params=PARAMS,
        name="add_shares",
    )

    def exchange(value):
        value = value.reshape(req_count, own_rows, width)
        value = lax.all_to_all(value, "req", split_axis=0, concat_axis=0, tiled=True)
        return value.reshape(patches, width)

    def section_step(current):
        everyone = exchange(norm(current, mod, *weights))
        partial_value = heads_and_units(
            everyone,
            *[pltpu.with_memory_space_constraint(weight, pltpu.VMEM) for weight in weights],
            stale,
            from_stale,
            bias,
        )
        return add_shares(exchange(partial_value), current, mod)

    onward = [(i, i + req_count) for i in range((section_count - 1) * req_count)]

    def at_turn(turn, current):
        return lax.cond(section_index == turn, section_step, lambda values: values, current)

    def advance(turn, current):
        return lax.ppermute(at_turn(turn, current), AXES, onward)

    current = lax.fori_loop(0, section_count - 1, advance, latents)
    current = at_turn(section_count - 1, current)
    pieces = current.reshape(own_rows, section_count, width // section_count).swapaxes(0, 1)
    pieces = lax.all_to_all(pieces, "section", split_axis=0, concat_axis=0, tiled=True)
    return pieces[section_count - 1]


def solution(mesh):
    in_specs = (
        P("req", None),
        P(),
        P(),
        P(),
        P("section", None, None, None),
        P("section", None, "req", None),
        P("section", None, "req"),
        P("section", "req", None, None),
        P("section", "req", None),
        P("section", None, "req", None),
    )
    out_specs = P("req", "section")
    return jax.shard_map(shards, mesh=mesh, in_specs=in_specs, out_specs=out_specs, check_vma=False)
```

time: 665 us -> 564 us (0.85)
  starting transfers between devices: 303 us -> 256 us
  blocking collectives: 288 us -> 248 us
  matrix products: 8.63 us -> 1.35 us
  waiting for transfers between devices: 57.5 us -> 50.5 us
    ppermute x16 -> x15, starting transfers between devices: 303 us -> 256 us  [advance(): return lax.ppermute(at_turn(turn, current), AXES, onward)]
    all_to_all x1, blocking collectives: 261 us -> 222 us  [shards(): lax.all_to_all(pieces, 'section', split_axis=0, concat_axis=0, tiled=True)]
    dot_general x6 -> x0, matrix products: 7.29 us -> none  [the longest x1 4.4 us: heads_and_units(): jnp.dot(mlp_act, mlp_out_weight, preferred_element_type=jnp.float32)]
    ppermute x16 -> x15, waiting for transfers between devices: 57.5 us -> 50.5 us  [advance(): return lax.ppermute(at_turn(turn, current), AXES, onward)]
  transfers between devices with their start and end apart: 16 -> 15, of which waited for: 16 -> 15; matrix products, arithmetic and copies ran while one was open for 0% -> 0% of each run, Pallas kernels for 0% -> 0%
where the time goes in v2:
time: 564 us; the launch traced here: 563 us
  starting transfers between devices  256 us (45%)
  blocking collectives  248 us (44%)
  waiting for transfers between devices  50.5 us (9%)
    ppermute x15, starting transfers between devices, advance(): return lax.ppermute(at_turn(turn, current), AXES, onward)  256 us
    all_to_all x1, blocking collectives, shards(): lax.all_to_all(pieces, 'section', split_axis=0, concat_axis=0, tiled=True)  222 us
    ppermute x15, waiting for transfers between devices, advance(): return lax.ppermute(at_turn(turn, current), AXES, onward)  50.5 us
    all_to_all x2, blocking collectives, exchange(): lax.all_to_all(value, 'req', split_axis=0, concat_axis=0, tiled=True)  26.4 us
  transfers between devices with their start and end apart: 15, of which 15 were waited for; matrix products, arithmetic and copies ran while one was open for 0% of the time, Pallas kernels for 0%

profile of v2, /device:TPU:1, one launch (start us, length us, event | category | flops | bytes accessed | tf_op | source)
XLA Modules:
  0.0 563.4 jit_solution(4940604208608060025)
XLA Ops:
  0.0 0.0 copy-start
  0.0 0.9 copy.33
  0.9 0.7 copy.16
  1.6 0.1 reduce
  1.8 0.7 sub.13
  2.4 0.1 convert_reduce_fusion
  2.5 0.1 compare_select_fusion
  2.6 0.1 dynamic_slice.3
  2.7 0.8 select_reduce_fusion
  3.4 1.0 convolution_convert_fusion
  4.5 0.0 copy-done
  4.5 0.3 convolution_bitcast_fusion
  4.8 0.7 fusion.7
  5.5 0.1 and_convert_fusion
  5.6 335.3 %while.19 = (s32[]{:T(128)}, bf16[8,3072]{1,0:T(8,128)(2,1)S(1)}, s32[]{:T(128)}, f32[3,8,3072]{2,1,0:T(8,128)S(1)}, bf16[3072,384]{1,0:T(8,128)(2,1)}, /*index=...) while((s32[]{:T(128)}, bf16[8,3072]{1,0:T(8,128)(2,1)S(1)}, ...), condition=%wide.region_6.7_spmd, body=%wide.region_3.6_spmd.sunk | while | flops 4 | bytes 34996584 | solution.py:199
  5.6 4.9 collective-permute-start
  10.5 34.3 %collective-permute-done = bf16[8,3072]{1,0:T(8,128)(2,1)S(1)} collective-permute-done((bf16[8,3072]{1,0:T(8,128)(2,1)S(1)}, bf16[8,3072]{1,0:T(8,128)(2,1)S(1)}, u32[]{:S(2)}, u32[]{:S(2)}) %collective-permute-start) | collective-permute-done | bytes 49184 | tf_op jit(solution)/shard_map/while/body/eval_jaxpr/ppermute | solution.py:197
  44.8 29.0 %conditional.4 = (bf16[8,3072]{1,0:T(8,128)(2,1)S(1)}) conditional(s32[]{:T(128)} %convert_element_type.29, bf16[8,3072]{1,0:T(8,128)(2,1)S(1)} %get-tuple-element.368, (bf16[8,3072]{1,0:T(8,128)(2,1)S(1)}, f32[3,8,3072]{2,1,0:T(8,128)S(1)}, bf16[3072,384]{1,0:T(8,128)(2,1)}, bf16[3072,384]{1,0:T(8,128)(2,1)}, bf16[128,3072]{1,0:T(8,128)(2,1)}, ...), branch_computations={%region_4.4_spmd, %region_5.5_spmd} | conditional | bytes 34701432 | solution.py:194
  44.8 0.0 copy-start.1
  44.8 0.0 copy-start.3
  44.9 0.0 copy-start.5
  44.9 0.0 copy-start.7
  44.9 0.3 spread_normed.2
  45.2 13.4 %all_to_all.21 = bf16[16,8,3072]{2,1,0:T(8,128)(2,1)S(1)} all-to-all(bf16[16,8,3072]{2,1,0:T(8,128)(2,1)S(1)} %bitcast.35), channel_id=1, replica_groups=mesh['section'=16,'req'=16] {'req'}, dimensions={0} | all-to-all | bytes 1572864 | tf_op jit(solution)/shard_map/while/body/eval_jaxpr/cond/branch_1_fun/all_to_all | solution.py:177
  58.6 0.0 copy-done.1
  58.6 0.0 copy-done.3
  58.6 0.0 copy-done.5
  58.6 0.0 copy-done.7
  58.6 2.1 heads_and_units.2
  60.7 13.0 %all_to_all.22 = bf16[16,8,3072]{2,1,0:T(8,128)(2,1)S(1)} all-to-all(bf16[16,8,3072]{2,1,0:T(8,128)(2,1)S(1)} %bitcast.34), channel_id=1, replica_groups=mesh['section'=16,'req'=16] {'req'}, dimensions={0} | all-to-all | bytes 1572864 | tf_op jit(solution)/shard_map/while/body/eval_jaxpr/cond/branch_1_fun/all_to_all | solution.py:177
  73.7 0.1 add_shares.2
  73.8 1.9 collective-permute-start
  75.8 1.2 collective-permute-done
  77.0 36.0 %collective-permute-start = (bf16[8,3072]{1,0:T(8,128)(2,1)S(1)}, bf16[8,3072]{1,0:T(8,128)(2,1)S(1)}, u32[]{:S(2)}, u32[]{:S(2)}) collective-permute-start(bf16[8,3072]{1,0:T(8,128)(2,1)S(1)} %get-tuple-element.392), channel_id=1, source_target_pairs={{0,16},{1,17},{2,18},{3,19},{4,20},{5,21},{6,22},{7,23},{8,24},{9,... | collective-permute-start | bytes 147464 | tf_op jit(solution)/shard_map/while/body/eval_jaxpr/ppermute | solution.py:197
  113.0 1.2 collective-permute-done
  114.1 4.2 collective-permute-start
  118.4 1.2 collective-permute-done
  119.5 28.4 %collective-permute-start = (bf16[8,3072]{1,0:T(8,128)(2,1)S(1)}, bf16[8,3072]{1,0:T(8,128)(2,1)S(1)}, u32[]{:S(2)}, u32[]{:S(2)}) collective-permute-start(bf16[8,3072]{1,0:T(8,128)(2,1)S(1)} %get-tuple-element.392), channel_id=1, source_target_pairs={{0,16},{1,17},{2,18},{3,19},{4,20},{5,21},{6,22},{7,23},{8,24},{9,... | collective-permute-start | bytes 147464 | tf_op jit(solution)/shard_map/while/body/eval_jaxpr/ppermute | solution.py:197
  147.9 1.2 collective-permute-done
  149.0 4.2 collective-permute-start
  153.3 1.2 collective-permute-done
  154.5 33.7 %collective-permute-start = (bf16[8,3072]{1,0:T(8,128)(2,1)S(1)}, bf16[8,3072]{1,0:T(8,128)(2,1)S(1)}, u32[]{:S(2)}, u32[]{:S(2)}) collective-permute-start(bf16[8,3072]{1,0:T(8,128)(2,1)S(1)} %get-tuple-element.392), channel_id=1, source_target_pairs={{0,16},{1,17},{2,18},{3,19},{4,20},{5,21},{6,22},{7,23},{8,24},{9,... | collective-permute-start | bytes 147464 | tf_op jit(solution)/shard_map/while/body/eval_jaxpr/ppermute | solution.py:197
  188.1 1.2 collective-permute-done
  189.3 4.2 collective-permute-start
  193.5 1.2 collective-permute-done
  194.7 28.4 %collective-permute-start = (bf16[8,3072]{1,0:T(8,128)(2,1)S(1)}, bf16[8,3072]{1,0:T(8,128)(2,1)S(1)}, u32[]{:S(2)}, u32[]{:S(2)}) collective-permute-start(bf16[8,3072]{1,0:T(8,128)(2,1)S(1)} %get-tuple-element.392), channel_id=1, source_target_pairs={{0,16},{1,17},{2,18},{3,19},{4,20},{5,21},{6,22},{7,23},{8,24},{9,... | collective-permute-start | bytes 147464 | tf_op jit(solution)/shard_map/while/body/eval_jaxpr/ppermute | solution.py:197
  223.1 1.2 collective-permute-done
  224.2 4.2 collective-permute-start
  228.5 1.2 collective-permute-done
  229.6 33.7 %collective-permute-start = (bf16[8,3072]{1,0:T(8,128)(2,1)S(1)}, bf16[8,3072]{1,0:T(8,128)(2,1)S(1)}, u32[]{:S(2)}, u32[]{:S(2)}) collective-permute-start(bf16[8,3072]{1,0:T(8,128)(2,1)S(1)} %get-tuple-element.392), channel_id=1, source_target_pairs={{0,16},{1,17},{2,18},{3,19},{4,20},{5,21},{6,22},{7,23},{8,24},{9,... | collective-permute-start | bytes 147464 | tf_op jit(solution)/shard_map/while/body/eval_jaxpr/ppermute | solution.py:197
  263.3 1.2 collective-permute-done
  264.5 4.2 collective-permute-start
  268.7 1.2 collective-permute-done
  269.9 28.4 %collective-permute-start = (bf16[8,3072]{1,0:T(8,128)(2,1)S(1)}, bf16[8,3072]{1,0:T(8,128)(2,1)S(1)}, u32[]{:S(2)}, u32[]{:S(2)}) collective-permute-start(bf16[8,3072]{1,0:T(8,128)(2,1)S(1)} %get-tuple-element.392), channel_id=1, source_target_pairs={{0,16},{1,17},{2,18},{3,19},{4,20},{5,21},{6,22},{7,23},{8,24},{9,... | collective-permute-start | bytes 147464 | tf_op jit(solution)/shard_map/while/body/eval_jaxpr/ppermute | solution.py:197
  298.3 1.2 collective-permute-done
  299.4 4.2 collective-permute-start
  303.7 1.2 collective-permute-done
  304.8 34.9 %collective-permute-start = (bf16[8,3072]{1,0:T(8,128)(2,1)S(1)}, bf16[8,3072]{1,0:T(8,128)(2,1)S(1)}, u32[]{:S(2)}, u32[]{:S(2)}) collective-permute-start(bf16[8,3072]{1,0:T(8,128)(2,1)S(1)} %get-tuple-element.392), channel_id=1, source_target_pairs={{0,16},{1,17},{2,18},{3,19},{4,20},{5,21},{6,22},{7,23},{8,24},{9,... | collective-permute-start | bytes 147464 | tf_op jit(solution)/shard_map/while/body/eval_jaxpr/ppermute | solution.py:197
  339.7 1.2 collective-permute-done
  340.9 0.1 reshape.102
  341.1 221.8 %all_to_all.25 = bf16[16,8,192]{2,1,0:T(8,128)(2,1)S(1)} all-to-all(bf16[16,8,192]{2,1,0:T(8,128)(2,1)S(1)} %copy.17), channel_id=1, replica_groups=mesh['section'=16,'req'=16] {'section'}, dimensions={0} | all-to-all | bytes 98304 | tf_op jit(solution)/shard_map/all_to_all | solution.py:202
  562.8 0.6 slice_bitcast_fusion
  (34 shorter events, 0.1 us)
Async XLA Ops:
  0.0 4.5 copy-start
  5.6 39.2 %collective-permute-start = (bf16[8,3072]{1,0:T(8,128)(2,1)S(1)}, bf16[8,3072]{1,0:T(8,128)(2,1)S(1)}, u32[]{:S(2)}, u32[]{:S(2)}) collective-permute-start(bf16[8,3072]{1,0:T(8,128)(2,1)S(1)} %get-tuple-element.392), channel_id=1, source_target_pairs={{0,16},{1,17},{2,18},{3,19},{4,20},{5,21},{6,22},{7,23},{8,24},{9,... | collective-permute-start | bytes 147464 | tf_op jit(solution)/shard_map/while/body/eval_jaxpr/ppermute | solution.py:197
  44.8 13.7 %copy-start.1 = (bf16[3072,384]{1,0:T(8,128)(2,1)S(1)}, bf16[3072,384]{1,0:T(8,128)(2,1)}, u32[]{:S(2)}) copy-start(bf16[3072,384]{1,0:T(8,128)(2,1)} %get-tuple-element.226.refs_0_.qkv_ref) | copy-start | bytes 7077892 | tf_op jit(solution)/shard_map/while/body/eval_jaxpr/cond
  44.8 13.7 %copy-start.3 = (bf16[3072,384]{1,0:T(8,128)(2,1)S(1)}, bf16[3072,384]{1,0:T(8,128)(2,1)}, u32[]{:S(2)}) copy-start(bf16[3072,384]{1,0:T(8,128)(2,1)} %get-tuple-element.227.refs_1_.mlp_ref) | copy-start | bytes 7077892 | tf_op jit(solution)/shard_map/while/body/eval_jaxpr/cond
  44.9 13.7 %copy-start.5 = (bf16[384,3072]{1,0:T(8,128)(2,1)S(1)}, bf16[384,3072]{1,0:T(8,128)(2,1)}, u32[]{:S(2)}) copy-start(bf16[384,3072]{1,0:T(8,128)(2,1)} %get-tuple-element.229.refs_3_.mlp_out_ref) | copy-start | bytes 7077892 | tf_op jit(solution)/shard_map/while/body/eval_jaxpr/cond
  44.9 13.7 %copy-start.7 = (bf16[128,3072]{1,0:T(8,128)(2,1)S(1)}, bf16[128,3072]{1,0:T(8,128)(2,1)}, u32[]{:S(2)}) copy-start(bf16[128,3072]{1,0:T(8,128)(2,1)} %get-tuple-element.228.refs_2_.attn_out_ref) | copy-start | bytes 2359300 | tf_op jit(solution)/shard_map/while/body/eval_jaxpr/cond
  73.8 3.1 collective-permute-start
  77.0 37.1 %collective-permute-start = (bf16[8,3072]{1,0:T(8,128)(2,1)S(1)}, bf16[8,3072]{1,0:T(8,128)(2,1)S(1)}, u32[]{:S(2)}, u32[]{:S(2)}) collective-permute-start(bf16[8,3072]{1,0:T(8,128)(2,1)S(1)} %get-tuple-element.392), channel_id=1, source_target_pairs={{0,16},{1,17},{2,18},{3,19},{4,20},{5,21},{6,22},{7,23},{8,24},{9,... | collective-permute-start | bytes 147464 | tf_op jit(solution)/shard_map/while/body/eval_jaxpr/ppermute | solution.py:197
  114.1 5.4 collective-permute-start
  119.5 29.5 %collective-permute-start = (bf16[8,3072]{1,0:T(8,128)(2,1)S(1)}, bf16[8,3072]{1,0:T(8,128)(2,1)S(1)}, u32[]{:S(2)}, u32[]{:S(2)}) collective-permute-start(bf16[8,3072]{1,0:T(8,128)(2,1)S(1)} %get-tuple-element.392), channel_id=1, source_target_pairs={{0,16},{1,17},{2,18},{3,19},{4,20},{5,21},{6,22},{7,23},{8,24},{9,... | collective-permute-start | bytes 147464 | tf_op jit(solution)/shard_map/while/body/eval_jaxpr/ppermute | solution.py:197
  149.0 5.4 collective-permute-start
  154.5 34.8 %collective-permute-start = (bf16[8,3072]{1,0:T(8,128)(2,1)S(1)}, bf16[8,3072]{1,0:T(8,128)(2,1)S(1)}, u32[]{:S(2)}, u32[]{:S(2)}) collective-permute-start(bf16[8,3072]{1,0:T(8,128)(2,1)S(1)} %get-tuple-element.392), channel_id=1, source_target_pairs={{0,16},{1,17},{2,18},{3,19},{4,20},{5,21},{6,22},{7,23},{8,24},{9,... | collective-permute-start | bytes 147464 | tf_op jit(solution)/shard_map/while/body/eval_jaxpr/ppermute | solution.py:197
  189.3 5.4 collective-permute-start
  194.7 29.5 %collective-permute-start = (bf16[8,3072]{1,0:T(8,128)(2,1)S(1)}, bf16[8,3072]{1,0:T(8,128)(2,1)S(1)}, u32[]{:S(2)}, u32[]{:S(2)}) collective-permute-start(bf16[8,3072]{1,0:T(8,128)(2,1)S(1)} %get-tuple-element.392), channel_id=1, source_target_pairs={{0,16},{1,17},{2,18},{3,19},{4,20},{5,21},{6,22},{7,23},{8,24},{9,... | collective-permute-start | bytes 147464 | tf_op jit(solution)/shard_map/while/body/eval_jaxpr/ppermute | solution.py:197
  224.2 5.4 collective-permute-start
  229.6 34.8 %collective-permute-start = (bf16[8,3072]{1,0:T(8,128)(2,1)S(1)}, bf16[8,3072]{1,0:T(8,128)(2,1)S(1)}, u32[]{:S(2)}, u32[]{:S(2)}) collective-permute-start(bf16[8,3072]{1,0:T(8,128)(2,1)S(1)} %get-tuple-element.392), channel_id=1, source_target_pairs={{0,16},{1,17},{2,18},{3,19},{4,20},{5,21},{6,22},{7,23},{8,24},{9,... | collective-permute-start | bytes 147464 | tf_op jit(solution)/shard_map/while/body/eval_jaxpr/ppermute | solution.py:197
  264.5 5.4 collective-permute-start
  269.9 29.5 %collective-permute-start = (bf16[8,3072]{1,0:T(8,128)(2,1)S(1)}, bf16[8,3072]{1,0:T(8,128)(2,1)S(1)}, u32[]{:S(2)}, u32[]{:S(2)}) collective-permute-start(bf16[8,3072]{1,0:T(8,128)(2,1)S(1)} %get-tuple-element.392), channel_id=1, source_target_pairs={{0,16},{1,17},{2,18},{3,19},{4,20},{5,21},{6,22},{7,23},{8,24},{9,... | collective-permute-start | bytes 147464 | tf_op jit(solution)/shard_map/while/body/eval_jaxpr/ppermute | solution.py:197
  299.4 5.4 collective-permute-start
  304.8 36.1 %collective-permute-start = (bf16[8,3072]{1,0:T(8,128)(2,1)S(1)}, bf16[8,3072]{1,0:T(8,128)(2,1)S(1)}, u32[]{:S(2)}, u32[]{:S(2)}) collective-permute-start(bf16[8,3072]{1,0:T(8,128)(2,1)S(1)} %get-tuple-element.392), channel_id=1, source_target_pairs={{0,16},{1,17},{2,18},{3,19},{4,20},{5,21},{6,22},{7,23},{8,24},{9,... | collective-permute-start | bytes 147464 | tf_op jit(solution)/shard_map/while/body/eval_jaxpr/ppermute | solution.py:197

commit v3 on v2

v3 whole, which is shorter than its diff:
```python
import functools

import jax
import jax.numpy as jnp
from jax import lax
from jax.experimental import pallas as pl
from jax.experimental.pallas import tpu as pltpu
from jax.sharding import PartitionSpec as P

AXES = ("section", "req")
BF16 = jnp.bfloat16
WIDTH_CUTS = 4
TILE = 16
VMEM = pl.BlockSpec(memory_space=pltpu.VMEM)
ANY = pl.BlockSpec(memory_space=pl.ANY)
PARAMS = pltpu.CompilerParams(vmem_limit_bytes=16 * 1024 * 1024)


def gelu_tanh(values):
    return (
        0.5
        * values
        * (1.0 + jnp.tanh(0.7978845608028654 * (values + 0.044715 * values * values * values)))
    )


def prepare_kernel(
    req_ref,
    span_hbm,
    route_hbm,
    len_hbm,
    modulation_hbm,
    stale_hbm,
    aux_ref,
    mod_ref,
    span_ref,
    route_ref,
    len_ref,
    modulation_ref,
    stale_ref,
    sems,
):
    moves = (
        (span_hbm, span_ref),
        (route_hbm, route_ref),
        (len_hbm, len_ref),
        (modulation_hbm, modulation_ref),
        (stale_hbm, stale_ref),
    )
    copies = [
        pltpu.make_async_copy(source, target, sems.at[i])
        for i, (source, target) in enumerate(moves)
    ]
    for copy in copies:
        copy.start()
    for copy in copies:
        copy.wait()
    patches = route_ref.shape[1]
    reqs = len_ref.shape[1]
    span_rows = patches // span_ref.shape[0]
    own_rows = mod_ref.shape[1]
    f32 = jnp.float32

    def down(rows, cols):
        return lax.broadcasted_iota(jnp.int32, (rows, cols), 0)

    def along(rows, cols):
        return lax.broadcasted_iota(jnp.int32, (rows, cols), 1)

    def total(mask, values, axis):
        return jnp.sum(jnp.where(mask, values, 0.0), axis=axis, keepdims=True)

    lens = jnp.broadcast_to(len_ref[...].astype(f32), (reqs, reqs))
    lens_down = total(down(reqs, reqs) == along(reqs, reqs), lens, 1)
    starts_along = total(down(reqs, reqs) < along(reqs, reqs), lens_down, 0)
    starts_down = total(along(reqs, reqs) < down(reqs, reqs), lens, 1)
    req_down = total(down(patches, reqs).astype(f32) >= starts_along, 1.0, 1) - 1.0
    req_along = total(along(reqs, patches).astype(f32) >= starts_down, 1.0, 0) - 1.0
    route = jnp.broadcast_to(route_ref[...], (patches, patches))
    square_down, square_along = down(patches, patches), along(patches, patches)
    at_position = square_down == route
    route_down = total(square_down == square_along, route.astype(f32), 1)
    position_down = total(at_position, square_along.astype(f32), 1)
    position_along = total(route_down == square_along.astype(f32), square_down.astype(f32), 0)
    first_row = (span_ref[0] * span_rows).astype(f32)

    def in_first(position):
        return (position >= first_row) & (position < first_row + span_rows)

    from_stale = jnp.where(in_first(position_down), 1.0, 0.0) * jnp.where(
        in_first(position_along), 0.0, 1.0
    )
    kind = jnp.where(req_down == req_along, 1.0 + from_stale, 0.0)
    stale_cols = stale_ref.shape[1]
    aux_ref[:, :stale_cols] = jnp.dot(
        jnp.where(at_position, 1.0, 0.0).astype(BF16),
        stale_ref[...],
        preferred_element_type=f32,
    ).astype(BF16)
    aux_ref[:, stale_cols:] = kind.astype(BF16)
    own = (down(own_rows, reqs) + req_ref[0] * own_rows).astype(f32)
    own_req = total(own >= starts_along, 1.0, 1) - 1.0
    for part in range(mod_ref.shape[0]):
        chosen = jnp.zeros(mod_ref.shape[1:], f32)
        for req in range(reqs):
            chosen = chosen + jnp.where(own_req == req, 1.0, 0.0) * modulation_ref[
                part, req : req + 1, :
            ]
        mod_ref[part] = chosen


def pack_kernel(qkv_ref, mlp_ref, attn_out_ref, mlp_out_ref, packed_ref, sems):
    width, qkv_cols = qkv_ref.shape
    head_dim, units = attn_out_ref.shape[0], mlp_out_ref.shape[0]
    cols = packed_ref.shape[1]
    moves = [
        (qkv_ref, packed_ref.at[pl.ds(0, width), pl.ds(0, qkv_cols)]),
        (mlp_ref, packed_ref.at[pl.ds(0, width), pl.ds(qkv_cols, units)]),
    ]
    for cut in range(width // cols):
        first = width + cut * (head_dim + units)
        span = pl.ds(cut * cols, cols)
        moves += [
            (attn_out_ref.at[:, span], packed_ref.at[pl.ds(first, head_dim), :]),
            (mlp_out_ref.at[:, span], packed_ref.at[pl.ds(first + head_dim, units), :]),
        ]
    copies = [
        pltpu.make_async_copy(source, target, sems.at[i])
        for i, (source, target) in enumerate(moves)
    ]
    for copy in copies:
        copy.start()
    for copy in copies:
        copy.wait()


def attend(qkv, aux_ref):
    head_dim = qkv.shape[1] // 3
    stale_cols = 2 * head_dim
    kind = aux_ref[:, stale_cols:]
    query, key, value = (
        qkv[:, :head_dim],
        qkv[:, head_dim : 2 * head_dim],
        qkv[:, 2 * head_dim :],
    )
    across = (((1,), (1,)), ((), ()))
    against_fresh = lax.dot_general(query, key, across, preferred_element_type=jnp.float32)
    against_stale = lax.dot_general(
        query, aux_ref[:, :head_dim], across, preferred_element_type=jnp.float32
    )
    kind = kind.astype(jnp.float32)
    from_stale = kind > 1.5
    scores = jnp.where(from_stale, against_stale, against_fresh) / jnp.sqrt(
        jnp.float32(head_dim)
    )
    scores = jnp.where(kind > 0.5, scores, -jnp.inf)
    exps = jnp.exp(scores - jnp.max(scores, axis=-1, keepdims=True))
    attention = exps / jnp.sum(exps, axis=-1, keepdims=True)
    attended = jnp.dot(
        jnp.where(from_stale, 0.0, attention).astype(BF16),
        value,
        preferred_element_type=jnp.float32,
    ) + jnp.dot(
        jnp.where(from_stale, attention, 0.0).astype(BF16),
        aux_ref[:, head_dim:stale_cols],
        preferred_element_type=jnp.float32,
    )
    return attended.astype(BF16)


def block_kernel(
    rows_ref,
    qkv_ref,
    mlp_ref,
    attn_out_ref,
    mlp_out_ref,
    aux_ref,
    out_ref,
):
    qkv = jnp.dot(rows_ref[...], qkv_ref[...], preferred_element_type=jnp.float32).astype(BF16)
    attended = attend(qkv, aux_ref)
    mlp_act = gelu_tanh(
        jnp.dot(rows_ref[...], mlp_ref[...], preferred_element_type=jnp.float32)
    ).astype(BF16)
    cols = out_ref.shape[1] // WIDTH_CUTS
    for cut in range(WIDTH_CUTS):
        span = slice(cut * cols, (cut + 1) * cols)
        out_ref[:, span] = (
            jnp.dot(attended, attn_out_ref[:, span], preferred_element_type=jnp.float32)
            + jnp.dot(mlp_act, mlp_out_ref[:, span], preferred_element_type=jnp.float32)
        ).astype(BF16)


def packed_block_kernel(qkv_cols, rows_ref, packed_ref, aux_ref, out_ref):
    width = rows_ref.shape[1]
    cols = packed_ref.shape[1]
    cuts = width // cols
    depth = (packed_ref.shape[0] - width) // cuts
    total = jnp.dot(
        rows_ref[...], packed_ref[:width, :], preferred_element_type=jnp.float32
    )
    attended = attend(total[:, :qkv_cols].astype(BF16), aux_ref)
    mlp_act = gelu_tanh(total[:, qkv_cols:]).astype(BF16)
    inner = jnp.concatenate([attended, mlp_act], axis=1)
    for cut in range(cuts):
        first = width + cut * depth
        out_ref[:, cut * cols : (cut + 1) * cols] = jnp.dot(
            inner, packed_ref[first : first + depth, :], preferred_element_type=jnp.float32
        ).astype(BF16)


def spread_normed(current, mod_ref, out_ref):
    row_mean = jnp.mean(current, axis=-1, keepdims=True)
    centered = current - row_mean
    row_var = jnp.mean(centered * centered, axis=-1, keepdims=True)
    normed = centered * lax.rsqrt(row_var + 1e-06) * (1.0 + mod_ref[1]) + mod_ref[0]
    twice = jnp.concatenate([normed, normed], axis=0).astype(BF16)
    for first in range(0, out_ref.shape[0], TILE):
        out_ref[first : first + TILE, :] = twice


def summed(shares_ref, current_ref, mod_ref):
    branch = shares_ref[:TILE, :].astype(jnp.float32)
    for first in range(TILE, shares_ref.shape[0], TILE):
        branch = branch + shares_ref[first : first + TILE, :].astype(jnp.float32)
    branch = branch[: TILE // 2] + branch[TILE // 2 :]
    return (current_ref[...].astype(jnp.float32) + mod_ref[2] * branch).astype(BF16)


def nothing_kernel(*refs):
    pass


def keep_kernel(*refs):
    for source, target in zip(refs[: len(refs) // 2], refs[len(refs) // 2 :]):
        target[...] = source[...]


def norm_kernel(current_ref, mod_ref, *refs):
    spread_normed(current_ref[...].astype(jnp.float32), mod_ref, refs[-1])


def sum_kernel(shares_ref, current_ref, mod_ref, out_ref):
    out_ref[...] = summed(shares_ref, current_ref, mod_ref)


def shards(
    latents,
    patch_route,
    request_len,
    span_order,
    modulation,
    w_qkv,
    w_mlp_in,
    w_out_attn,
    w_out_mlp,
    stale_kv,
):
    section_count = lax.axis_size("section")
    req_count = lax.axis_size("req")
    section_index = lax.axis_index("section")
    req_index = lax.axis_index("req")
    patches = patch_route.shape[0]
    own_rows, width = latents.shape
    qkv_cols = w_qkv.shape[3]
    head_dim = w_out_attn.shape[2]
    units = w_mlp_in.shape[2]

    near = pl.BlockSpec(memory_space=pltpu.SMEM)
    operands = (
        span_order,
        patch_route.reshape(1, patches),
        request_len.reshape(1, -1),
        modulation[0].swapaxes(0, 1),
        stale_kv[0, :, 0],
    )
    aux, mod = pl.pallas_call(
        prepare_kernel,
        out_shape=(
            pltpu.VMEM((patches, 2 * head_dim + patches), BF16),
            pltpu.VMEM((3, own_rows, width), jnp.float32),
        ),
        in_specs=[near] + [ANY] * 5,
        out_specs=(VMEM, VMEM),
        scratch_shapes=[pltpu.SMEM(span_order.shape, span_order.dtype)]
        + [pltpu.VMEM(value.shape, value.dtype) for value in operands[1:]]
        + [pltpu.SemaphoreType.DMA((5,))],
        compiler_params=PARAMS,
        name="prepare",
    )(req_index.astype(jnp.int32).reshape(1), *operands)
    mod, aux = lax.optimization_barrier((mod, aux))
    own_weights = (w_qkv[0, :, 0], w_mlp_in[0], w_out_attn[0, 0], w_out_mlp[0])
    to_sibling = [
        (i, i + req_count)
        for i in range(2 * req_count, section_count * req_count)
        if i // req_count % 2 == 0
    ]
    packed_cols = qkv_cols + units
    pack = pl.pallas_call(
        pack_kernel,
        out_shape=jax.ShapeDtypeStruct(
            (width + width // packed_cols * (head_dim + units), packed_cols), BF16
        ),
        in_specs=[ANY] * 4,
        out_specs=VMEM,
        compiler_params=PARAMS,
        scratch_shapes=[pltpu.SemaphoreType.DMA((2 + 2 * (width // packed_cols),))],
        name="pack_weights",
    )

    def chip_sections(weights, aux, mod):
        own = (pack(*weights), aux, mod)
        return own[0], *(lax.ppermute(value, AXES, to_sibling) for value in own)

    def unused(function):
        def nothing(*values):
            shapes, tree = jax.tree.flatten(jax.eval_shape(function, *values))
            results = pl.pallas_call(
                nothing_kernel,
                out_shape=tuple(jax.ShapeDtypeStruct(v.shape, v.dtype) for v in shapes),
                out_specs=(ANY,) * len(shapes),
                name="unused",
            )()
            return jax.tree.unflatten(tree, results)

        return nothing

    all_rows = jax.ShapeDtypeStruct((patches, width), BF16)
    own = jax.ShapeDtypeStruct((own_rows, width), BF16)
    def norm(current, mod, *weights):
        return pl.pallas_call(
            norm_kernel,
            out_shape=all_rows,
            in_specs=[VMEM] * 2 + [ANY] * len(weights),
            out_specs=VMEM,
            compiler_params=PARAMS,
            name="spread_normed",
        )(current, mod, *weights)

    def heads_and_units(everyone, weights, aux):
        kernel = block_kernel
        if len(weights) == 1:
            kernel = functools.partial(packed_block_kernel, qkv_cols)
        return pl.pallas_call(
            kernel,
            out_shape=all_rows,
            in_specs=[VMEM] * (2 + len(weights)),
            out_specs=VMEM,
            compiler_params=PARAMS,
            name="heads_and_units",
        )(
            everyone,
            *[pltpu.with_memory_space_constraint(value, pltpu.VMEM) for value in weights],
            aux,
        )

    add_shares = pl.pallas_call(
        sum_kernel,
        out_shape=own,
        in_specs=[VMEM] * 3,
        out_specs=VMEM,
        compiler_params=PARAMS,
        name="add_shares",
    )

    def exchange(value):
        value = value.reshape(req_count, own_rows, width)
        value = lax.all_to_all(value, "req", split_axis=0, concat_axis=0, tiled=True)
        return value.reshape(patches, width)

    def one_section(current, *section):
        *weights, aux, mod = section
        everyone = exchange(norm(current, mod, *weights, aux))
        partial_value = heads_and_units(everyone, weights, aux)
        return add_shares(exchange(partial_value), current, mod)

    def when(section, current, held):
        return lax.cond(
            section_index == section, one_section, unused(one_section), current, *held
        )

    def hand_over(current, sections):
        pairs = [(a * req_count + i, b * req_count + i) for a, b in sections for i in range(req_count)]
        return lax.ppermute(current, AXES, pairs)

    def chip_turn(chip, current):
        current = when(2 * chip + 1, current, first_held)
        return when(2 * chip + 1, current, second_held)

    onward = [(section, section + 2) for section in range(1, section_count - 1, 2)]
    current = when(0, latents, (*own_weights, aux, mod))
    current = hand_over(current, [(0, 1)])
    current = when(1, current, (*own_weights, aux, mod))
    current = hand_over(current, onward)
    own_packed, *first_held = lax.cond(
        section_index >= 2, chip_sections, unused(chip_sections), own_weights, aux, mod
    )
    own_packed, first_packed = (
        jnp.where(section_index >= 2, value, jnp.zeros_like(value))
        for value in (own_packed, first_held[0])
    )
    small = pl.pallas_call(
        keep_kernel,
        out_shape=tuple(pltpu.VMEM(value.shape, value.dtype) for value in (aux, mod)),
        in_specs=[VMEM] * 2,
        out_specs=(VMEM, VMEM),
        compiler_params=PARAMS,
        name="keep",
    )(*first_held[1:])
    first_held = (first_packed, *small)
    second_held = (own_packed, aux, mod)
    last = section_count // 2 - 1
    current = lax.fori_loop(
        1, last, lambda chip, rows: hand_over(chip_turn(chip, rows), onward), current
    )
    current = chip_turn(last, current)
    pieces = current.reshape(own_rows, section_count, width // section_count).swapaxes(0, 1)
    pieces = lax.all_to_all(pieces, "section", split_axis=0, concat_axis=0, tiled=True)
    return pieces[section_count - 1]


def solution(mesh):
    in_specs = (
        P("req", None),
        P(),
        P(),
        P(),
        P("section", None, None, None),
        P("section", None, "req", None),
        P("section", None, "req"),
        P("section", "req", None, None),
        P("section", "req", None),
        P("section", None, "req", None),
    )
    out_specs = P("req", "section")
    return jax.shard_map(shards, mesh=mesh, in_specs=in_specs, out_specs=out_specs, check_vma=False)
```

time: 564 us -> 518 us (0.918)
  starting transfers between devices: 256 us -> 187 us
  blocking collectives: 248 us -> 266 us
    ppermute x15 -> x8, starting transfers between devices: 256 us -> 187 us  [hand_over(): return lax.ppermute(current, AXES, pairs)]
    all_to_all x1, blocking collectives: 222 us -> 240 us  [shards(): lax.all_to_all(pieces, 'section', split_axis=0, concat_axis=0, tiled=True)]
    select_n x1, other arithmetic: 0.08 us -> 5.77 us  [shards(): jnp.where(section_index >= 2, value, jnp.zeros_like(value))]
    ppermute x15 -> x8, waiting for transfers between devices: 50.5 us -> 45.9 us  [hand_over(): return lax.ppermute(current, AXES, pairs)]
  transfers between devices with their start and end apart: 15 -> 8, of which waited for: 15 -> 7; matrix products, arithmetic and copies ran while one was open for 0% -> 1% of each run, Pallas kernels for 0% -> 0%
where the time goes in v3:
time: 518 us; the launch traced here: 517 us
  blocking collectives  266 us (51%)
  starting transfers between devices  187 us (36%)
  waiting for transfers between devices  45.9 us (9%)
  Pallas kernels  7.21 us (1%)
  other arithmetic  5.77 us (1%)
    all_to_all x1, blocking collectives, shards(): lax.all_to_all(pieces, 'section', split_axis=0, concat_axis=0, tiled=True)  240 us
    ppermute x8, starting transfers between devices, hand_over(): return lax.ppermute(current, AXES, pairs)  187 us
    ppermute x8, waiting for transfers between devices, hand_over(): return lax.ppermute(current, AXES, pairs)  45.9 us
    all_to_all x2, blocking collectives, exchange(): lax.all_to_all(value, 'req', split_axis=0, concat_axis=0, tiled=True)  26.3 us
  transfers between devices with their start and end apart: 8, of which 7 were waited for; matrix products, arithmetic and copies ran while one was open for 1% of the time, Pallas kernels for 0%

profile of v3, /device:TPU:1, one launch (start us, length us, event | category | flops | bytes accessed | tf_op | source)
XLA Modules:
  0.0 517.1 jit_solution(8846861821136661410)
XLA Ops:
  0.0 0.0 copy-start.12
  0.0 1.1 copy-done.12
  1.1 0.0 copy-start.13
  1.1 0.8 copy-done.13
  1.9 0.0 copy-start.14
  1.9 0.7 copy-done.14
  2.6 0.0 copy-start.15
  2.6 0.7 copy-done.15
  3.2 0.0 copy-start.16
  3.2 0.7 copy-done.16
  3.9 1.3 prepare.1
  5.2 1.3 collective-permute-start.4
  6.5 39.0 %collective-permute-done.4 = bf16[8,3072]{1,0:T(8,128)(2,1)} collective-permute-done((bf16[8,3072]{1,0:T(8,128)(2,1)S(1)}, bf16[8,3072]{1,0:T(8,128)(2,1)}, u32[]{:S(2)}, u32[]{:S(2)}) %collective-permute-start.4) | collective-permute-done | bytes 49184 | tf_op jit(solution)/shard_map/ppermute | solution.py:384
  45.5 31.2 %conditional.8 = (bf16[8,3072]{1,0:T(8,128)(2,1)}) conditional(s32[]{:T(128)} %convert_element_type.22, () %tuple.65, (bf16[8,3072]{1,0:T(8,128)(2,1)}, f32[3,8,3072]{2,1,0:T(8,128)S(1)}, bf16[3072,384]{1,0:T(8,128)(2,1)}, bf16[3072,384]{1,0:T(8,128)(2,1)}, bf16[128,3072]{1,0:T(8,128)(2,1)}, /*index=5*/bf16[384,3072]{1,0:T(8,128)(2,1)}, ...), branch_computations={%region_2.0_spmd, %region_3.0_spmd} | conditional | bytes 34603128 | solution.py:378
  45.5 0.0 copy-start.5
  45.5 0.0 copy-start.7
  45.5 0.0 copy-start.9
  45.5 0.0 copy-start.11
  45.5 1.2 spread_normed.7
  46.7 13.3 %all_to_all.55 = bf16[16,8,3072]{2,1,0:T(8,128)(2,1)S(1)} all-to-all(bf16[16,8,3072]{2,1,0:T(8,128)(2,1)S(1)} %bitcast.67), channel_id=1, replica_groups=mesh['section'=16,'req'=16] {'req'}, dimensions={0} | all-to-all | bytes 1572864 | tf_op jit(solution)/shard_map/cond/branch_1_fun/all_to_all | solution.py:368
  60.0 0.0 copy-done.5
  60.0 0.0 copy-done.7
  60.0 0.0 copy-done.9
  60.0 0.0 copy-done.11
  60.0 2.1 heads_and_units.7
  62.2 13.0 %all_to_all.56 = bf16[16,8,3072]{2,1,0:T(8,128)(2,1)S(1)} all-to-all(bf16[16,8,3072]{2,1,0:T(8,128)(2,1)S(1)} %bitcast.61), channel_id=1, replica_groups=mesh['section'=16,'req'=16] {'req'}, dimensions={0} | all-to-all | bytes 1572864 | tf_op jit(solution)/shard_map/cond/branch_1_fun/all_to_all | solution.py:368
  75.2 1.5 add_shares.7
  76.7 1.5 collective-permute-start.5
  78.2 5.8 %broadcast_select_fusion = (bf16[5120,768]{1,0:T(8,128)(2,1)}, bf16[5120,768]{1,0:T(8,128)(2,1)}) fusion(bf16[5120,768]{1,0:T(8,128)(2,1)} %get-tuple-element.312, pred[]{:T(512)S(6)} %ge.2, bf16[5120,768]{1,0:T(8,128)(2,1)} %get-tuple-element.310), kind=kLoop, calls=%fused_computation | loop fusion | flops 7864320 | bytes 31457280 | tf_op jit(solution)/shard_map/jit(_where)/select_n | solution.py:399
  83.9 1.0 keep.1
  85.0 0.0 collective-permute-done.5
  85.0 191.3 %while.13 = (s32[]{:T(128)}, bf16[8,3072]{1,0:T(8,128)(2,1)S(1)}, s32[]{:T(128)}, f32[3,8,3072]{2,1,0:T(8,128)S(1)}, bf16[5120,768]{1,0:T(8,128)(2,1)}, /*index=...) while((s32[]{:T(128)}, bf16[8,3072]{1,0:T(8,128)(2,1)S(1)}, ...), condition=%wide.region_11.12_spmd, body=%wide.region_6.11_spmd.sunk | while | flops 6 | bytes 69402952 | solution.py:413
  85.1 55.1 %collective-permute-start.3 = (bf16[8,3072]{1,0:T(8,128)(2,1)S(1)}, bf16[8,3072]{1,0:T(8,128)(2,1)S(1)}, u32[]{:S(2)}, u32[]{:S(2)}) collective-permute-start(bf16[8,3072]{1,0:T(8,128)(2,1)S(1)} %get-tuple-element.438), channel_id=1, source_target_pairs={{16,48},{17,49},{18,50},{19,51},{20,52},{21,53},{22,54},{23,55},{2... | collective-permute-start | bytes 147464 | tf_op jit(solution)/shard_map/while/body/eval_jaxpr/ppermute | solution.py:384
  140.2 1.2 collective-permute-done.3
  141.3 3.7 collective-permute-start.3
  145.0 1.2 collective-permute-done.3
  146.2 59.1 %collective-permute-start.3 = (bf16[8,3072]{1,0:T(8,128)(2,1)S(1)}, bf16[8,3072]{1,0:T(8,128)(2,1)S(1)}, u32[]{:S(2)}, u32[]{:S(2)}) collective-permute-start(bf16[8,3072]{1,0:T(8,128)(2,1)S(1)} %get-tuple-element.438), channel_id=1, source_target_pairs={{16,48},{17,49},{18,50},{19,51},{20,52},{21,53},{22,54},{23,55},{2... | collective-permute-start | bytes 147464 | tf_op jit(solution)/shard_map/while/body/eval_jaxpr/ppermute | solution.py:384
  205.2 1.2 collective-permute-done.3
  206.4 3.7 collective-permute-start.3
  210.1 1.2 collective-permute-done.3
  211.2 59.1 %collective-permute-start.3 = (bf16[8,3072]{1,0:T(8,128)(2,1)S(1)}, bf16[8,3072]{1,0:T(8,128)(2,1)S(1)}, u32[]{:S(2)}, u32[]{:S(2)}) collective-permute-start(bf16[8,3072]{1,0:T(8,128)(2,1)S(1)} %get-tuple-element.438), channel_id=1, source_target_pairs={{16,48},{17,49},{18,50},{19,51},{20,52},{21,53},{22,54},{23,55},{2... | collective-permute-start | bytes 147464 | tf_op jit(solution)/shard_map/while/body/eval_jaxpr/ppermute | solution.py:384
  270.3 1.2 collective-permute-done.3
  271.5 3.7 collective-permute-start.3
  275.1 1.2 collective-permute-done.3
  276.3 0.1 reshape.87
  276.5 240.1 %all_to_all.65 = bf16[16,8,192]{2,1,0:T(8,128)(2,1)S(1)} all-to-all(bf16[16,8,192]{2,1,0:T(8,128)(2,1)S(1)} %copy.12), channel_id=1, replica_groups=mesh['section'=16,'req'=16] {'section'}, dimensions={0} | all-to-all | bytes 98304 | tf_op jit(solution)/shard_map/all_to_all | solution.py:418
  516.5 0.6 slice_bitcast_fusion
  (33 shorter events, 0.1 us)
Async XLA Ops:
  0.0 1.1 copy-start.12
  1.1 0.8 copy-start.13
  1.9 0.7 copy-start.14
  2.6 0.7 copy-start.15
  3.2 0.7 copy-start.16
  5.2 40.3 %collective-permute-start.4 = (bf16[8,3072]{1,0:T(8,128)(2,1)S(1)}, bf16[8,3072]{1,0:T(8,128)(2,1)}, u32[]{:S(2)}, u32[]{:S(2)}) collective-permute-start(bf16[8,3072]{1,0:T(8,128)(2,1)S(1)} %get-tuple-element.432), channel_id=1, source_target_pairs={{0,16},{1,17},{2,18},{3,19},{4,20},{5,21},{6,22},{7,23},{8,24},{9,... | collective-permute-start | bytes 147464 | tf_op jit(solution)/shard_map/ppermute | solution.py:384
  45.5 14.5 %copy-start.5 = (bf16[3072,384]{1,0:T(8,128)(2,1)S(1)}, bf16[3072,384]{1,0:T(8,128)(2,1)}, u32[]{:S(2)}) copy-start(bf16[3072,384]{1,0:T(8,128)(2,1)} %get-tuple-element.255.refs_0_.qkv_ref) | copy-start | bytes 7077892 | tf_op jit(solution)/shard_map/cond
  45.5 14.5 %copy-start.7 = (bf16[3072,384]{1,0:T(8,128)(2,1)S(1)}, bf16[3072,384]{1,0:T(8,128)(2,1)}, u32[]{:S(2)}) copy-start(bf16[3072,384]{1,0:T(8,128)(2,1)} %get-tuple-element.256.refs_1_.mlp_ref) | copy-start | bytes 7077892 | tf_op jit(solution)/shard_map/cond
  45.5 14.5 %copy-start.9 = (bf16[384,3072]{1,0:T(8,128)(2,1)S(1)}, bf16[384,3072]{1,0:T(8,128)(2,1)}, u32[]{:S(2)}) copy-start(bf16[384,3072]{1,0:T(8,128)(2,1)} %get-tuple-element.258.refs_3_.mlp_out_ref) | copy-start | bytes 7077892 | tf_op jit(solution)/shard_map/cond
  45.5 14.5 %copy-start.11 = (bf16[128,3072]{1,0:T(8,128)(2,1)S(1)}, bf16[128,3072]{1,0:T(8,128)(2,1)}, u32[]{:S(2)}) copy-start(bf16[128,3072]{1,0:T(8,128)(2,1)} %get-tuple-element.257.refs_2_.attn_out_ref) | copy-start | bytes 2359300 | tf_op jit(solution)/shard_map/cond
  76.7 8.3 %collective-permute-start.5 = (bf16[8,3072]{1,0:T(8,128)(2,1)}, bf16[8,3072]{1,0:T(8,128)(2,1)S(1)}, u32[]{:S(2)}, u32[]{:S(2)}) collective-permute-start(bf16[8,3072]{1,0:T(8,128)(2,1)} %get-tuple-element.433), channel_id=1, source_target_pairs={{16,48},{17,49},{18,50},{19,51},{20,52},{21,53},{22,54},{23,55},{2... | collective-permute-start | bytes 147464 | tf_op jit(solution)/shard_map/ppermute | solution.py:384
  85.1 56.3 %collective-permute-start.3 = (bf16[8,3072]{1,0:T(8,128)(2,1)S(1)}, bf16[8,3072]{1,0:T(8,128)(2,1)S(1)}, u32[]{:S(2)}, u32[]{:S(2)}) collective-permute-start(bf16[8,3072]{1,0:T(8,128)(2,1)S(1)} %get-tuple-element.438), channel_id=1, source_target_pairs={{16,48},{17,49},{18,50},{19,51},{20,52},{21,53},{22,54},{23,55},{2... | collective-permute-start | bytes 147464 | tf_op jit(solution)/shard_map/while/body/eval_jaxpr/ppermute | solution.py:384
  141.3 4.8 collective-permute-start.3
  146.2 60.2 %collective-permute-start.3 = (bf16[8,3072]{1,0:T(8,128)(2,1)S(1)}, bf16[8,3072]{1,0:T(8,128)(2,1)S(1)}, u32[]{:S(2)}, u32[]{:S(2)}) collective-permute-start(bf16[8,3072]{1,0:T(8,128)(2,1)S(1)} %get-tuple-element.438), channel_id=1, source_target_pairs={{16,48},{17,49},{18,50},{19,51},{20,52},{21,53},{22,54},{23,55},{2... | collective-permute-start | bytes 147464 | tf_op jit(solution)/shard_map/while/body/eval_jaxpr/ppermute | solution.py:384
  206.4 4.8 collective-permute-start.3
  211.2 60.2 %collective-permute-start.3 = (bf16[8,3072]{1,0:T(8,128)(2,1)S(1)}, bf16[8,3072]{1,0:T(8,128)(2,1)S(1)}, u32[]{:S(2)}, u32[]{:S(2)}) collective-permute-start(bf16[8,3072]{1,0:T(8,128)(2,1)S(1)} %get-tuple-element.438), channel_id=1, source_target_pairs={{16,48},{17,49},{18,50},{19,51},{20,52},{21,53},{22,54},{23,55},{2... | collective-permute-start | bytes 147464 | tf_op jit(solution)/shard_map/while/body/eval_jaxpr/ppermute | solution.py:384
  271.5 4.8 collective-permute-start.3

commit v4 on v3

--- a/solution.py
+++ b/solution.py
@@ -13,6 +13,7 @@
 TILE = 16
 VMEM = pl.BlockSpec(memory_space=pltpu.VMEM)
 ANY = pl.BlockSpec(memory_space=pl.ANY)
+LARGE = pltpu.CompilerParams(vmem_limit_bytes=58 * 1024 * 1024)
 PARAMS = pltpu.CompilerParams(vmem_limit_bytes=16 * 1024 * 1024)
 
 
@@ -136,36 +137,26 @@
 
 def attend(qkv, aux_ref):
     head_dim = qkv.shape[1] // 3
+    rows = qkv.shape[0]
     stale_cols = 2 * head_dim
-    kind = aux_ref[:, stale_cols:]
-    query, key, value = (
-        qkv[:, :head_dim],
-        qkv[:, head_dim : 2 * head_dim],
-        qkv[:, 2 * head_dim :],
-    )
-    across = (((1,), (1,)), ((), ()))
-    against_fresh = lax.dot_general(query, key, across, preferred_element_type=jnp.float32)
-    against_stale = lax.dot_general(
-        query, aux_ref[:, :head_dim], across, preferred_element_type=jnp.float32
-    )
-    kind = kind.astype(jnp.float32)
+    query = qkv[:, :head_dim]
+    keys = jnp.concatenate([qkv[:, head_dim:stale_cols], aux_ref[:, :head_dim]], axis=0)
+    values = jnp.concatenate([qkv[:, stale_cols:], aux_ref[:, head_dim:stale_cols]], axis=0)
+    kind = aux_ref[:, stale_cols:].astype(jnp.float32)
     from_stale = kind > 1.5
-    scores = jnp.where(from_stale, against_stale, against_fresh) / jnp.sqrt(
+    both = lax.dot_general(
+        query, keys, (((1,), (1,)), ((), ())), preferred_element_type=jnp.float32
+    )
+    scores = jnp.where(from_stale, both[:, rows:], both[:, :rows]) / jnp.sqrt(
         jnp.float32(head_dim)
     )
     scores = jnp.where(kind > 0.5, scores, -jnp.inf)
     exps = jnp.exp(scores - jnp.max(scores, axis=-1, keepdims=True))
-    attention = exps / jnp.sum(exps, axis=-1, keepdims=True)
-    attended = jnp.dot(
-        jnp.where(from_stale, 0.0, attention).astype(BF16),
-        value,
-        preferred_element_type=jnp.float32,
-    ) + jnp.dot(
-        jnp.where(from_stale, attention, 0.0).astype(BF16),
-        aux_ref[:, head_dim:stale_cols],
-        preferred_element_type=jnp.float32,
-    )
-    return attended.astype(BF16)
+    weights = jnp.concatenate(
+        [jnp.where(from_stale, 0.0, exps), jnp.where(from_stale, exps, 0.0)], axis=1
+    ).astype(BF16)
+    attended = jnp.dot(weights, values, preferred_element_type=jnp.float32)
+    return (attended / jnp.sum(exps, axis=-1, keepdims=True)).astype(BF16)
 
 
 def block_kernel(
@@ -231,9 +222,17 @@
     pass
 
 
-def keep_kernel(*refs):
-    for source, target in zip(refs[: len(refs) // 2], refs[len(refs) // 2 :]):
-        target[...] = source[...]
+def keep_kernel(section_ref, aux_hbm, mod_hbm, aux_ref, mod_ref, sems):
+    @pl.when(section_ref[0] >= 2)
+    def _():
+        copies = [
+            pltpu.make_async_copy(aux_hbm, aux_ref, sems.at[0]),
+            pltpu.make_async_copy(mod_hbm, mod_ref, sems.at[1]),
+        ]
+        for copy in copies:
+            copy.start()
+        for copy in copies:
+            copy.wait()
 
 
 def norm_kernel(current_ref, mod_ref, *refs):
@@ -285,7 +284,7 @@
         scratch_shapes=[pltpu.SMEM(span_order.shape, span_order.dtype)]
         + [pltpu.VMEM(value.shape, value.dtype) for value in operands[1:]]
         + [pltpu.SemaphoreType.DMA((5,))],
-        compiler_params=PARAMS,
+        compiler_params=LARGE,
         name="prepare",
     )(req_index.astype(jnp.int32).reshape(1), *operands)
     mod, aux = lax.optimization_barrier((mod, aux))
@@ -387,32 +386,41 @@
         current = when(2 * chip + 1, current, first_held)
         return when(2 * chip + 1, current, second_held)
 
-    onward = [(section, section + 2) for section in range(1, section_count - 1, 2)]
-    current = when(0, latents, (*own_weights, aux, mod))
-    current = hand_over(current, [(0, 1)])
-    current = when(1, current, (*own_weights, aux, mod))
-    current = hand_over(current, onward)
+    start = (*own_weights, aux, mod)
+    current = lax.fori_loop(
+        0, 2, lambda section, rows: hand_over(when(section, rows, start), [(0, 1), (1, 3)]), latents
+    )
     own_packed, *first_held = lax.cond(
         section_index >= 2, chip_sections, unused(chip_sections), own_weights, aux, mod
     )
-    own_packed, first_packed = (
-        jnp.where(section_index >= 2, value, jnp.zeros_like(value))
-        for value in (own_packed, first_held[0])
-    )
+    own_packed, first_packed = pl.pallas_call(
+        nothing_kernel,
+        out_shape=(jax.ShapeDtypeStruct(own_packed.shape, BF16),) * 2,
+        in_specs=[ANY] * 2,
+        out_specs=(ANY,) * 2,
+        input_output_aliases={0: 0, 1: 1},
+        name="pass_on",
+    )(own_packed, first_held[0])
     small = pl.pallas_call(
         keep_kernel,
         out_shape=tuple(pltpu.VMEM(value.shape, value.dtype) for value in (aux, mod)),
-        in_specs=[VMEM] * 2,
+        in_specs=[near] + [ANY] * 2,
         out_specs=(VMEM, VMEM),
-        compiler_params=PARAMS,
+        scratch_shapes=[pltpu.SemaphoreType.DMA((2,))],
+        compiler_params=LARGE,
         name="keep",
-    )(*first_held[1:])
+    )(section_index.astype(jnp.int32).reshape(1), *first_held[1:])
     first_held = (first_packed, *small)
     second_held = (own_packed, aux, mod)
     last = section_count // 2 - 1
-    current = lax.fori_loop(
-        1, last, lambda chip, rows: hand_over(chip_turn(chip, rows), onward), current
-    )
+    onward = [[(2 * c + 1, 2 * c + 3) for c in range(first, last, 2)] for first in (1, 2)]
+
+    def two_chips(turn, current):
+        for i, pairs in enumerate(onward):
+            current = hand_over(chip_turn(2 * turn + 1 + i, current), pairs)
+        return current
+
+    current = lax.fori_loop(0, last // 2, two_chips, current)
     current = chip_turn(last, current)
     pieces = current.reshape(own_rows, section_count, width // section_count).swapaxes(0, 1)
     pieces = lax.all_to_all(pieces, "section", split_axis=0, concat_axis=0, tiled=True)

time: 518 us -> 507 us (0.979)
  blocking collectives: 266 us -> 453 us
  starting transfers between devices: 187 us -> 34.9 us
  waiting for transfers between devices: 45.9 us -> 11.3 us
  other arithmetic: 5.77 us -> 0 us
    all_to_all x1, blocking collectives: 240 us -> 427 us  [shards(): lax.all_to_all(pieces, 'section', split_axis=0, concat_axis=0, tiled=True)]
    ppermute x8, starting transfers between devices: 187 us -> 34.9 us  [hand_over(): return lax.ppermute(current, AXES, pairs)]
    ppermute x8, waiting for transfers between devices: 45.9 us -> 11.3 us  [hand_over(): return lax.ppermute(current, AXES, pairs)]
    select_n x1 -> x0, other arithmetic: 5.77 us -> none  [shards(): jnp.where(section_index >= 2, value, jnp.zeros_like(value))]
  transfers between devices with their start and end apart: 8 -> 8, of which waited for: 7 -> 2; matrix products, arithmetic and copies ran while one was open for 1% -> 0% of each run, Pallas kernels for 0% -> 0%
where the time goes in v4:
time: 507 us
  blocking collectives  453 us (89%)
  starting transfers between devices  34.9 us (7%)
  waiting for transfers between devices  11.3 us (2%)
    all_to_all x1, blocking collectives, shards(): lax.all_to_all(pieces, 'section', split_axis=0, concat_axis=0, tiled=True)  427 us
    ppermute x8, starting transfers between devices, hand_over(): return lax.ppermute(current, AXES, pairs)  34.9 us
    all_to_all x2, blocking collectives, exchange(): lax.all_to_all(value, 'req', split_axis=0, concat_axis=0, tiled=True)  26.3 us
    ppermute x8, waiting for transfers between devices, hand_over(): return lax.ppermute(current, AXES, pairs)  11.3 us
  transfers between devices with their start and end apart: 8, of which 2 were waited for; matrix products, arithmetic and copies ran while one was open for 0% of the time, Pallas kernels for 0%

profile of v4, /device:TPU:1, one launch (start us, length us, event | category | flops | bytes accessed | tf_op | source)
XLA Modules:
  0.0 506.8 jit_solution(14657831877663523813)
XLA Ops:
  0.0 1.8 prepare.1
  1.9 0.0 copy-start.8
  1.9 0.0 copy-start.12
  1.9 1.6 copy-done.8
  3.5 0.0 copy-done.12
  3.5 70.9 %while.28 = (s32[]{:T(128)}, bf16[8,3072]{1,0:T(8,128)(2,1)S(1)}, s32[]{:T(128)}, f32[3,8,3072]{2,1,0:T(8,128)S(1)}, bf16[3072,384]{1,0:T(8,128)(2,1)S(1)}, /*in...) while((s32[]{:T(128)}, bf16[8,3072]{1,0:T(8,128)(2,1)S(1)}, ...), condition=%wide.region_3.0_spmd, body=%wide.region_0.0_spmd.sunk | while | flops 4 | bytes 25362736 | solution.py:390
  3.5 29.0 %collective-permute-start.3 = (bf16[8,3072]{1,0:T(8,128)(2,1)S(1)}, bf16[8,3072]{1,0:T(8,128)(2,1)S(1)}, u32[]{:S(2)}, u32[]{:S(2)}) collective-permute-start(bf16[8,3072]{1,0:T(8,128)(2,1)S(1)} %get-tuple-element.789), channel_id=1, source_target_pairs={{0,16},{1,17},{2,18},{3,19},{4,20},{5,21},{6,22},{7,23},{8,24},{9,... | collective-permute-start | bytes 147464 | tf_op jit(solution)/shard_map/while/body/eval_jaxpr/ppermute | solution.py:383
  32.5 10.1 %collective-permute-done.3 = bf16[8,3072]{1,0:T(8,128)(2,1)S(1)} collective-permute-done((bf16[8,3072]{1,0:T(8,128)(2,1)S(1)}, bf16[8,3072]{1,0:T(8,128)(2,1)S(1)}, u32[]{:S(2)}, u32[]{:S(2)}) %collective-permute-start.3) | collective-permute-done | bytes 49184 | tf_op jit(solution)/shard_map/while/body/eval_jaxpr/ppermute | solution.py:383
  42.6 28.8 %conditional.16 = (bf16[8,3072]{1,0:T(8,128)(2,1)S(1)}) conditional(s32[]{:T(128)} %convert_element_type.41, () %tuple.125, (bf16[8,3072]{1,0:T(8,128)(2,1)S(1)}, f32[3,8,3072]{2,1,0:T(8,128)S(1)}, bf16[3072,384]{1,0:T(8,128)(2,1)S(1)}, bf16[3072,384]{1,0:T(8,128)(2,1)}, bf16[128,3072]{1,0:T(8,128)(2,1)}, /*index=5*/bf16[384,3072]{1,0:T(8,128)(2,1)}, ...), branch_computations={%region_1.0_spmd, %region_2.0_spmd} | conditional | bytes 25165916 | solution.py:377
  42.6 0.0 copy-start.9
  42.6 0.0 copy-start.10
  42.6 0.0 copy-start.11
  42.6 0.3 spread_normed.7
  42.9 13.3 %all_to_all.61 = bf16[16,8,3072]{2,1,0:T(8,128)(2,1)S(1)} all-to-all(bf16[16,8,3072]{2,1,0:T(8,128)(2,1)S(1)} %bitcast.61), channel_id=1, replica_groups=mesh['section'=16,'req'=16] {'req'}, dimensions={0} | all-to-all | bytes 1572864 | tf_op jit(solution)/shard_map/while/body/eval_jaxpr/cond/branch_1_fun/all_to_all | solution.py:367
  56.2 0.0 copy-done.9
  56.2 0.0 copy-done.10
  56.2 0.0 copy-done.11
  56.2 2.0 heads_and_units.7
  58.2 13.0 %all_to_all.62 = bf16[16,8,3072]{2,1,0:T(8,128)(2,1)S(1)} all-to-all(bf16[16,8,3072]{2,1,0:T(8,128)(2,1)S(1)} %bitcast.52), channel_id=1, replica_groups=mesh['section'=16,'req'=16] {'req'}, dimensions={0} | all-to-all | bytes 1572864 | tf_op jit(solution)/shard_map/while/body/eval_jaxpr/cond/branch_1_fun/all_to_all | solution.py:367
  71.2 0.1 add_shares.7
  71.4 1.9 collective-permute-start.3
  73.3 1.2 collective-permute-done.3
  74.5 4.5 while.29
  74.5 0.7 collective-permute-start.4
  75.2 0.0 collective-permute-done.4
  75.2 0.7 collective-permute-start.5
  75.9 0.0 collective-permute-done.5
  76.0 0.7 collective-permute-start.4
  76.7 0.0 collective-permute-done.4
  76.7 0.7 collective-permute-start.5
  77.4 0.0 collective-permute-done.5
  77.5 0.7 collective-permute-start.4
  78.2 0.0 collective-permute-done.4
  78.3 0.7 collective-permute-start.5
  78.9 0.0 collective-permute-done.5
  79.0 0.2 conditional.9
  79.2 0.1 reshape.103
  79.4 426.8 %all_to_all.75 = bf16[16,8,192]{2,1,0:T(8,128)(2,1)S(1)} all-to-all(bf16[16,8,192]{2,1,0:T(8,128)(2,1)S(1)} %copy.13), channel_id=1, replica_groups=mesh['section'=16,'req'=16] {'section'}, dimensions={0} | all-to-all | bytes 98304 | tf_op jit(solution)/shard_map/all_to_all | solution.py:426
  506.2 0.6 slice_bitcast_fusion
  (34 shorter events, 0.3 us)
Async XLA Ops:
  1.9 1.7 copy-start.8
  1.9 1.7 copy-start.12
  3.5 39.1 %collective-permute-start.3 = (bf16[8,3072]{1,0:T(8,128)(2,1)S(1)}, bf16[8,3072]{1,0:T(8,128)(2,1)S(1)}, u32[]{:S(2)}, u32[]{:S(2)}) collective-permute-start(bf16[8,3072]{1,0:T(8,128)(2,1)S(1)} %get-tuple-element.789), channel_id=1, source_target_pairs={{0,16},{1,17},{2,18},{3,19},{4,20},{5,21},{6,22},{7,23},{8,24},{9,... | collective-permute-start | bytes 147464 | tf_op jit(solution)/shard_map/while/body/eval_jaxpr/ppermute | solution.py:383
  42.6 13.6 %copy-start.9 = (bf16[3072,384]{1,0:T(8,128)(2,1)S(1)}, bf16[3072,384]{1,0:T(8,128)(2,1)}, u32[]{:S(2)}) copy-start(bf16[3072,384]{1,0:T(8,128)(2,1)} %get-tuple-element.487.refs_1_.mlp_ref) | copy-start | bytes 7077892 | tf_op jit(solution)/shard_map/while/body/eval_jaxpr/cond
  42.6 13.6 %copy-start.10 = (bf16[384,3072]{1,0:T(8,128)(2,1)S(1)}, bf16[384,3072]{1,0:T(8,128)(2,1)}, u32[]{:S(2)}) copy-start(bf16[384,3072]{1,0:T(8,128)(2,1)} %get-tuple-element.489.refs_3_.mlp_out_ref) | copy-start | bytes 7077892 | tf_op jit(solution)/shard_map/while/body/eval_jaxpr/cond
  42.6 13.6 %copy-start.11 = (bf16[128,3072]{1,0:T(8,128)(2,1)S(1)}, bf16[128,3072]{1,0:T(8,128)(2,1)}, u32[]{:S(2)}) copy-start(bf16[128,3072]{1,0:T(8,128)(2,1)} %get-tuple-element.488.refs_2_.attn_out_ref) | copy-start | bytes 2359300 | tf_op jit(solution)/shard_map/while/body/eval_jaxpr/cond
  71.4 3.1 collective-permute-start.3
  74.5 0.7 collective-permute-start.4
  75.2 0.7 collective-permute-start.5
  76.0 0.7 collective-permute-start.4
  76.7 0.7 collective-permute-start.5
  77.5 0.7 collective-permute-start.4
  78.3 0.7 collective-permute-start.5

commit v5 on v4

--- a/solution.py
+++ b/solution.py
@@ -11,6 +11,9 @@
 BF16 = jnp.bfloat16
 WIDTH_CUTS = 4
 TILE = 16
+HELD = 10
+LANES = 128
+SECOND = 48
 VMEM = pl.BlockSpec(memory_space=pltpu.VMEM)
 ANY = pl.BlockSpec(memory_space=pl.ANY)
 LARGE = pltpu.CompilerParams(vmem_limit_bytes=58 * 1024 * 1024)
@@ -23,6 +26,79 @@
         * values
         * (1.0 + jnp.tanh(0.7978845608028654 * (values + 0.044715 * values * values * values)))
     )
+
+
+def down(rows, cols):
+    return lax.broadcasted_iota(jnp.int32, (rows, cols), 0)
+
+
+def along(rows, cols):
+    return lax.broadcasted_iota(jnp.int32, (rows, cols), 1)
+
+
+def total(mask, values, axis):
+    return jnp.sum(jnp.where(mask, values, 0.0), axis=axis, keepdims=True)
+
+
+def request_starts(len_ref):
+    reqs = len_ref.shape[1]
+    lens = jnp.broadcast_to(len_ref[...].astype(jnp.float32), (reqs, reqs))
+    lens_down = total(down(reqs, reqs) == along(reqs, reqs), lens, 1)
+    return (
+        total(down(reqs, reqs) < along(reqs, reqs), lens_down, 0),
+        total(along(reqs, reqs) < down(reqs, reqs), lens, 1),
+    )
+
+
+def write_aux(aux_ref, row_of, span_ref, route_ref, len_ref, stale_ref):
+    patches, reqs = route_ref.shape[1], len_ref.shape[1]
+    rows, stale_cols = aux_ref.shape[0], stale_ref.shape[1]
+    places = aux_ref.shape[1] - stale_cols
+    span_rows = patches // span_ref.shape[0]
+    f32 = jnp.float32
+    starts_along, starts_down = request_starts(len_ref)
+    row_down = row_of(down(rows, reqs)).astype(f32)
+    row_along = row_of(along(reqs, places)).astype(f32)
+    req_down = total(row_down >= starts_along, 1.0, 1) - 1.0
+    req_along = total(row_along >= starts_down, 1.0, 0) - 1.0
+    route = jnp.broadcast_to(route_ref[...], (patches, patches))
+    route_down = total(down(patches, patches) == along(patches, patches), route.astype(f32), 1)
+    at_position = row_of(down(rows, patches)) == jnp.broadcast_to(
+        route_ref[...], (rows, patches)
+    )
+    position_down = total(at_position, along(rows, patches).astype(f32), 1)
+    position_along = total(
+        route_down == row_of(along(patches, places)).astype(f32),
+        down(patches, places).astype(f32),
+        0,
+    )
+    first_row = (span_ref[0] * span_rows).astype(f32)
+
+    def in_first(position):
+        return (position >= first_row) & (position < first_row + span_rows)
+
+    from_stale = jnp.where(in_first(position_down), 1.0, 0.0) * jnp.where(
+        in_first(position_along), 0.0, 1.0
+    )
+    counts = jnp.where(along(rows, places) < rows, 1.0, 0.0)
+    kind = jnp.where(req_down == req_along, (1.0 + from_stale) * counts, 0.0)
+    aux_ref[:, :stale_cols] = jnp.dot(
+        jnp.where(at_position, 1.0, 0.0).astype(BF16),
+        stale_ref[...],
+        preferred_element_type=f32,
+    ).astype(BF16)
+    aux_ref[:, stale_cols:] = kind.astype(BF16)
+
+
+def fetch(pairs, sems):
+    copies = [
+        pltpu.make_async_copy(source, target, sems.at[i])
+        for i, (source, target) in enumerate(pairs)
+    ]
+    for copy in copies:
+        copy.start()
+    for copy in copies:
+        copy.wait()
 
 
 def prepare_kernel(
@@ -41,73 +117,131 @@
     stale_ref,
     sems,
 ):
-    moves = (
-        (span_hbm, span_ref),
-        (route_hbm, route_ref),
-        (len_hbm, len_ref),
-        (modulation_hbm, modulation_ref),
-        (stale_hbm, stale_ref),
-    )
-    copies = [
-        pltpu.make_async_copy(source, target, sems.at[i])
-        for i, (source, target) in enumerate(moves)
-    ]
-    for copy in copies:
-        copy.start()
-    for copy in copies:
-        copy.wait()
-    patches = route_ref.shape[1]
-    reqs = len_ref.shape[1]
-    span_rows = patches // span_ref.shape[0]
-    own_rows = mod_ref.shape[1]
-    f32 = jnp.float32
-
-    def down(rows, cols):
-        return lax.broadcasted_iota(jnp.int32, (rows, cols), 0)
-
-    def along(rows, cols):
-        return lax.broadcasted_iota(jnp.int32, (rows, cols), 1)
-
-    def total(mask, values, axis):
-        return jnp.sum(jnp.where(mask, values, 0.0), axis=axis, keepdims=True)
-
-    lens = jnp.broadcast_to(len_ref[...].astype(f32), (reqs, reqs))
-    lens_down = total(down(reqs, reqs) == along(reqs, reqs), lens, 1)
-    starts_along = total(down(reqs, reqs) < along(reqs, reqs), lens_down, 0)
-    starts_down = total(along(reqs, reqs) < down(reqs, reqs), lens, 1)
-    req_down = total(down(patches, reqs).astype(f32) >= starts_along, 1.0, 1) - 1.0
-    req_along = total(along(reqs, patches).astype(f32) >= starts_down, 1.0, 0) - 1.0
-    route = jnp.broadcast_to(route_ref[...], (patches, patches))
-    square_down, square_along = down(patches, patches), along(patches, patches)
-    at_position = square_down == route
-    route_down = total(square_down == square_along, route.astype(f32), 1)
-    position_down = total(at_position, square_along.astype(f32), 1)
-    position_along = total(route_down == square_along.astype(f32), square_down.astype(f32), 0)
-    first_row = (span_ref[0] * span_rows).astype(f32)
-
-    def in_first(position):
-        return (position >= first_row) & (position < first_row + span_rows)
-
-    from_stale = jnp.where(in_first(position_down), 1.0, 0.0) * jnp.where(
-        in_first(position_along), 0.0, 1.0
-    )
-    kind = jnp.where(req_down == req_along, 1.0 + from_stale, 0.0)
-    stale_cols = stale_ref.shape[1]
-    aux_ref[:, :stale_cols] = jnp.dot(
-        jnp.where(at_position, 1.0, 0.0).astype(BF16),
-        stale_ref[...],
-        preferred_element_type=f32,
-    ).astype(BF16)
-    aux_ref[:, stale_cols:] = kind.astype(BF16)
-    own = (down(own_rows, reqs) + req_ref[0] * own_rows).astype(f32)
-    own_req = total(own >= starts_along, 1.0, 1) - 1.0
+    fetch(
+        (
+            (span_hbm, span_ref),
+            (route_hbm, route_ref),
+            (len_hbm, len_ref),
+            (modulation_hbm, modulation_ref),
+            (stale_hbm, stale_ref),
+        ),
+        sems,
+    )
+    write_aux(aux_ref, lambda place: place, span_ref, route_ref, len_ref, stale_ref)
+    reqs, own_rows = len_ref.shape[1], mod_ref.shape[1]
+    own = (down(own_rows, reqs) + req_ref[0] * own_rows).astype(jnp.float32)
+    own_req = total(own >= request_starts(len_ref)[0], 1.0, 1) - 1.0
     for part in range(mod_ref.shape[0]):
-        chosen = jnp.zeros(mod_ref.shape[1:], f32)
+        chosen = jnp.zeros(mod_ref.shape[1:], jnp.float32)
         for req in range(reqs):
             chosen = chosen + jnp.where(own_req == req, 1.0, 0.0) * modulation_ref[
                 part, req : req + 1, :
             ]
         mod_ref[part] = chosen
+
+
+def fold(rows):
+    cols = rows[0].shape[1] // 8
+    return jnp.concatenate(
+        [
+            jnp.concatenate([row[:, s * cols : (s + 1) * cols] for s in range(8)], axis=0)
+            for row in rows
+        ],
+        axis=1,
+    )
+
+
+def prepare_half_kernel(
+    req_ref,
+    span_hbm,
+    route_hbm,
+    len_hbm,
+    modulation_hbm,
+    stale_hbm,
+    mine_ref,
+    theirs_ref,
+    mod_ref,
+    span_ref,
+    route_ref,
+    len_ref,
+    modulation_ref,
+    stale_ref,
+    sems,
+):
+    fetch(
+        (
+            (span_hbm, span_ref),
+            (route_hbm, route_ref),
+            (len_hbm, len_ref),
+            (modulation_hbm, modulation_ref),
+            (stale_hbm, stale_ref),
+        ),
+        sems,
+    )
+    base = jnp.where(req_ref[0] >= 8, SECOND, 0)
+    seat = jnp.bitwise_and(req_ref[0], 7)
+    for first, aux_ref in ((base, mine_ref), (SECOND - base, theirs_ref)):
+
+        def row_of(place):
+            return first + jnp.bitwise_and(place, 7) * HELD + lax.shift_right_logical(place, 3)
+
+        write_aux(aux_ref, row_of, span_ref, route_ref, len_ref, stale_ref)
+    reqs = len_ref.shape[1]
+    held = (down(16, reqs) + base + seat * HELD).astype(jnp.float32)
+    held_req = total(held >= request_starts(len_ref)[0], 1.0, 1) - 1.0
+    for part in range(mod_ref.shape[0]):
+        chosen = jnp.zeros((16, modulation_ref.shape[2]), jnp.float32)
+        for req in range(reqs):
+            chosen = chosen + jnp.where(held_req == req, 1.0, 0.0) * modulation_ref[
+                part, req : req + 1, :
+            ]
+        mod_ref[part] = fold([chosen[i : i + 1] for i in range(HELD)])
+
+
+def same_kernel(values_ref, out_ref):
+    out_ref[...] = values_ref[...]
+
+
+def fold_kernel(req_ref, first_ref, second_ref, out_ref):
+    skipped = jnp.bitwise_and(jnp.bitwise_and(req_ref[0], 7) * HELD, 7)
+    rows = jnp.concatenate(
+        [first_ref[...].astype(jnp.float32), second_ref[...].astype(jnp.float32)], axis=0
+    ).astype(BF16)
+    pick = jnp.where(along(16, 16) == down(16, 16) + skipped, 1.0, 0.0).astype(BF16)
+    picked = jnp.dot(pick, rows, preferred_element_type=jnp.float32)
+    out_ref[...] = fold([picked[i : i + 1] for i in range(HELD)]).astype(BF16)
+
+
+def unfold_kernel(current_ref, out_ref):
+    cols = current_ref.shape[1] // HELD
+    current = current_ref[...].astype(jnp.float32)
+    rows = [
+        jnp.concatenate(
+            [current[s : s + 1, i * cols : (i + 1) * cols] for s in range(8)], axis=1
+        )
+        for i in range(HELD)
+    ]
+    rows.append(jnp.zeros((out_ref.shape[0] - HELD, 8 * cols), jnp.float32))
+    out_ref[...] = jnp.concatenate(rows, axis=0).astype(BF16)
+
+
+def place_kernel(req_ref, rows_ref, len_ref, out_ref):
+    patches, held = out_ref.shape[0], rows_ref.shape[0]
+    base = jnp.where(req_ref[0] >= 8, SECOND, 0)
+    held_first = base + jnp.bitwise_and(req_ref[0], 7) * HELD
+    starts, _ = request_starts(len_ref)
+    ends = starts + len_ref[...].astype(jnp.float32)
+    border = jnp.max(jnp.where(ends <= 8 * HELD, ends, 0.0), axis=1, keepdims=True)
+    place = down(patches, held)
+    before = place.astype(jnp.float32) < border
+    first_half = jnp.where(base == 0, 1.0, 0.0)
+    counts = jnp.where(before, first_half, 1.0 - first_half)
+    here = jnp.where(
+        (place == held_first + along(patches, held)) & (along(patches, held) < HELD), counts, 0.0
+    )
+    out_ref[...] = jnp.dot(
+        here.astype(BF16), rows_ref[...], preferred_element_type=jnp.float32
+    ).astype(BF16)
 
 
 def pack_kernel(qkv_ref, mlp_ref, attn_out_ref, mlp_out_ref, packed_ref, sems):
@@ -139,15 +273,23 @@
     head_dim = qkv.shape[1] // 3
     rows = qkv.shape[0]
     stale_cols = 2 * head_dim
+    places = aux_ref.shape[1] - stale_cols
+
+    def both_kinds(fresh, stale):
+        if rows == places:
+            return jnp.concatenate([fresh, stale], axis=0)
+        none = jnp.zeros((places - rows, head_dim), BF16)
+        return jnp.concatenate([fresh, none, stale, none], axis=0)
+
     query = qkv[:, :head_dim]
-    keys = jnp.concatenate([qkv[:, head_dim:stale_cols], aux_ref[:, :head_dim]], axis=0)
-    values = jnp.concatenate([qkv[:, stale_cols:], aux_ref[:, head_dim:stale_cols]], axis=0)
+    keys = both_kinds(qkv[:, head_dim:stale_cols], aux_ref[:, :head_dim])
+    values = both_kinds(qkv[:, stale_cols:], aux_ref[:, head_dim:stale_cols])
     kind = aux_ref[:, stale_cols:].astype(jnp.float32)
     from_stale = kind > 1.5
     both = lax.dot_general(
         query, keys, (((1,), (1,)), ((), ())), preferred_element_type=jnp.float32
     )
-    scores = jnp.where(from_stale, both[:, rows:], both[:, :rows]) / jnp.sqrt(
+    scores = jnp.where(from_stale, both[:, places:], both[:, :places]) / jnp.sqrt(
         jnp.float32(head_dim)
     )
     scores = jnp.where(kind > 0.5, scores, -jnp.inf)
@@ -200,6 +342,100 @@
         ).astype(BF16)
 
 
+def half_block_kernel(
+    qkv_cols,
+    rows_ref,
+    packed_ref,
+    their_packed_hbm,
+    aux_ref,
+    their_aux_ref,
+    out_ref,
+    their_packed_ref,
+    spread_ref,
+    inputs_ref,
+    sems,
+):
+    width = inputs_ref.shape[1]
+    rest = packed_ref.shape[0] - width
+    reads = [
+        pltpu.make_async_copy(
+            their_packed_hbm.at[pl.ds(first, count), :],
+            their_packed_ref.at[pl.ds(first, count), :],
+            sems.at[i],
+        )
+        for i, (first, count) in enumerate(((0, width), (width, rest)))
+    ]
+    for read in reads:
+        read.start()
+    piece = width // 8
+    cols = packed_ref.shape[1]
+    cuts = width // cols
+    depth = (packed_ref.shape[0] - width) // cuts
+    tiles = piece // LANES
+    for tile in range(spread_ref.shape[0]):
+        spread_ref[tile] = rows_ref[:, tile * LANES : (tile + 1) * LANES].astype(jnp.float32)
+    for i in range(0, HELD, 2):
+        for s in range(8):
+            for t in range(tiles):
+                inputs_ref[
+                    8 * i : 8 * i + 16, s * piece + t * LANES : s * piece + (t + 1) * LANES
+                ] = jnp.concatenate(
+                    [spread_ref[k * tiles + t, pl.ds(s, 8, stride=8), :] for k in (i, i + 1)],
+                    axis=0,
+                ).astype(BF16)
+    sums = [
+        jnp.dot(inputs_ref[...], packed_ref[:width, :], preferred_element_type=jnp.float32)
+    ]
+    reads[0].wait()
+    sums.append(
+        jnp.dot(inputs_ref[...], their_packed_ref[:width, :], preferred_element_type=jnp.float32)
+    )
+    inner = []
+    for values, extra in zip(sums, (aux_ref, their_aux_ref)):
+        attended = attend(values[:, :qkv_cols].astype(BF16), extra)
+        mlp_act = gelu_tanh(values[:, qkv_cols:]).astype(BF16)
+        inner.append(jnp.concatenate([attended, mlp_act], axis=1))
+    reads[1].wait()
+    for cut in range(cuts):
+        first = width + cut * depth
+        out = jnp.dot(
+            inner[0], packed_ref[first : first + depth, :], preferred_element_type=jnp.float32
+        ) + jnp.dot(
+            inner[1],
+            their_packed_ref[first : first + depth, :],
+            preferred_element_type=jnp.float32,
+        )
+        for k in range(cols // piece):
+            s = cut * (cols // piece) + k
+            for i in range(HELD):
+                for t in range(tiles):
+                    first = k * piece + t * LANES
+                    spread_ref[i * tiles + t, pl.ds(s, 8, stride=8), :] = out[
+                        8 * i : 8 * i + 8, first : first + LANES
+                    ]
+    for tile in range(spread_ref.shape[0]):
+        out_ref[:, tile * LANES : (tile + 1) * LANES] = spread_ref[tile].astype(BF16)
+
+
+def of_row(values):
+    return jnp.sum(jnp.sum(values, axis=1, keepdims=True), axis=0, keepdims=True)
+
+
+def half_norm_kernel(current_ref, mod_ref, *refs):
+    out_ref = refs[-1]
+    current = current_ref[...].astype(jnp.float32)
+    cols = current.shape[1] // HELD
+    normed = []
+    for i in range(HELD):
+        values = current[:, i * cols : (i + 1) * cols]
+        centered = values - of_row(values) / (8 * cols)
+        normed.append(centered * lax.rsqrt(of_row(centered * centered) / (8 * cols) + 1e-06))
+    normed = jnp.concatenate(normed, axis=1) * (1.0 + mod_ref[1]) + mod_ref[0]
+    twice = jnp.concatenate([normed, normed], axis=0).astype(BF16)
+    for first in range(0, out_ref.shape[0], TILE):
+        out_ref[first : first + TILE, :] = twice
+
+
 def spread_normed(current, mod_ref, out_ref):
     row_mean = jnp.mean(current, axis=-1, keepdims=True)
     centered = current - row_mean
@@ -222,17 +458,13 @@
     pass
 
 
-def keep_kernel(section_ref, aux_hbm, mod_hbm, aux_ref, mod_ref, sems):
-    @pl.when(section_ref[0] >= 2)
+def keep_kernel(least, section_ref, *refs):
+    *refs, sems = refs
+    count = len(refs) // 2
+
+    @pl.when(section_ref[0] >= least)
     def _():
-        copies = [
-            pltpu.make_async_copy(aux_hbm, aux_ref, sems.at[0]),
-            pltpu.make_async_copy(mod_hbm, mod_ref, sems.at[1]),
-        ]
-        for copy in copies:
-            copy.start()
-        for copy in copies:
-            copy.wait()
+        fetch(list(zip(refs[:count], refs[count:])), sems)
 
 
 def norm_kernel(current_ref, mod_ref, *refs):
@@ -382,49 +614,222 @@
         pairs = [(a * req_count + i, b * req_count + i) for a, b in sections for i in range(req_count)]
         return lax.ppermute(current, AXES, pairs)
 
-    def chip_turn(chip, current):
+    start = (*own_weights, aux, mod)
+    current = hand_over(when(0, latents, start), [(0, 1)])
+    current = hand_over(when(1, current, start), [(1, 3)])
+
+    def settle(least, packed, small):
+        packed = pl.pallas_call(
+            nothing_kernel,
+            out_shape=tuple(jax.ShapeDtypeStruct(value.shape, BF16) for value in packed),
+            in_specs=[ANY] * len(packed),
+            out_specs=(ANY,) * len(packed),
+            input_output_aliases={i: i for i in range(len(packed))},
+            name="pass_on",
+        )(*packed)
+        small = pl.pallas_call(
+            functools.partial(keep_kernel, least),
+            out_shape=tuple(pltpu.VMEM(value.shape, value.dtype) for value in small),
+            in_specs=[near] + [ANY] * len(small),
+            out_specs=(VMEM,) * len(small),
+            scratch_shapes=[pltpu.SemaphoreType.DMA((len(small),))],
+            compiler_params=LARGE,
+            name="keep",
+        )(section_index.astype(jnp.int32).reshape(1), *small)
+        return packed, small
+
+    own_packed, *first = lax.cond(
+        section_index >= 2, chip_sections, unused(chip_sections), own_weights, aux, mod
+    )
+    (own_packed, first_packed), small = settle(2, (own_packed, first[0]), first[1:])
+    first_held, own_held = (first_packed, *small), (own_packed, aux, mod)
+
+    early = section_count // 4
+    req_id = req_index.astype(jnp.int32).reshape(1)
+    side = 4
+    partner = [(side - 1 - r // side) * side + r % side for r in range(req_count)]
+    window = (8 * HELD, 2 * head_dim + patches)
+    folded = (8, HELD * width // 8)
+
+    def late_sections(own_packed, first_packed, *operands):
+        mine, theirs, mods = pl.pallas_call(
+            prepare_half_kernel,
+            out_shape=(
+                jax.ShapeDtypeStruct(window, BF16),
+                jax.ShapeDtypeStruct(window, BF16),
+                jax.ShapeDtypeStruct((3, *folded), jnp.float32),
+            ),
+            in_specs=[near] + [ANY] * 5,
+            out_specs=(VMEM,) * 3,
+            scratch_shapes=[pltpu.SMEM(span_order.shape, span_order.dtype)]
+            + [pltpu.VMEM(value.shape, value.dtype) for value in operands[1:]]
+            + [pltpu.SemaphoreType.DMA((5,))],
+            compiler_params=PARAMS,
+            name="prepare_half",
+        )(req_id, *operands)
+        own = (mine, theirs, mods)
+        pairs = [
+            (i, i + req_count)
+            for i in range(2 * early * req_count, section_count * req_count)
+            if i // req_count % 2 == 0
+        ]
+        first = tuple(lax.ppermute(value, AXES, pairs) for value in own)
+        swap = [
+            (s * req_count + r, s * req_count + partner[r])
+            for s in range(2 * early + 1, section_count, 2)
+            for r in range(req_count)
+        ]
+        swapped = tuple(
+            lax.ppermute(value, AXES, swap)
+            for value in (first[1], own[1], first_packed, own_packed)
+        )
+        return (*swapped[2:], first[0], swapped[0], first[2], own[0], swapped[1], own[2])
+
+    late = lax.cond(
+        section_index >= 2 * early,
+        late_sections,
+        unused(late_sections),
+        own_packed,
+        first_packed,
+        *operands,
+    )
+    their_packed, small = settle(2 * early, late[:2], late[2:])
+    first_half = (first_packed, their_packed[0], *small[:3])
+    own_half = (own_packed, their_packed[1], *small[3:])
+
+    def half_step(current, packed, their_packed, aux, their_aux, mod):
+        rows = jax.ShapeDtypeStruct((8 * 8, folded[1]), BF16)
+        halves = [list(range(8)), list(range(8, 16))]
+
+        def exchange(value):
+            value = value.reshape(8, *folded)
+            value = lax.all_to_all(
+                value, "req", split_axis=0, concat_axis=0, tiled=True, axis_index_groups=halves
+            )
+            return value.reshape(rows.shape)
+
+        spread = pl.pallas_call(
+            half_norm_kernel,
+            out_shape=rows,
+            in_specs=[VMEM] * 2 + [ANY] * 3,
+            out_specs=VMEM,
+            compiler_params=PARAMS,
+            name="half_spread_normed",
+        )(current, mod, packed, aux, their_aux)
+        partial_value = pl.pallas_call(
+            functools.partial(half_block_kernel, qkv_cols),
+            out_shape=rows,
+            in_specs=[VMEM] * 2 + [ANY] + [VMEM] * 2,
+            out_specs=VMEM,
+            scratch_shapes=[
+                pltpu.VMEM(packed.shape, BF16),
+                pltpu.VMEM((folded[1] // LANES, rows.shape[0], LANES), jnp.float32),
+                pltpu.VMEM((window[0], width), BF16),
+                pltpu.SemaphoreType.DMA((2,)),
+            ],
+            compiler_params=pltpu.CompilerParams(vmem_limit_bytes=24 * 1024 * 1024),
+            name="half_heads_and_units",
+        )(
+            exchange(spread),
+            pltpu.with_memory_space_constraint(packed, pltpu.VMEM),
+            their_packed,
+            aux,
+            their_aux,
+        )
+        return pl.pallas_call(
+            sum_kernel,
+            out_shape=jax.ShapeDtypeStruct(folded, BF16),
+            in_specs=[VMEM] * 3,
+            out_specs=VMEM,
+            compiler_params=PARAMS,
+            name="half_add_shares",
+        )(exchange(partial_value), current, mod)
+
+    def turn(chip, current):
         current = when(2 * chip + 1, current, first_held)
-        return when(2 * chip + 1, current, second_held)
-
-    start = (*own_weights, aux, mod)
+        return when(2 * chip + 1, current, own_held)
+
+    def late_turn(chip, current):
+        for held in (first_half, own_half):
+            current = lax.cond(
+                section_index == 2 * chip + 1, half_step, unused(half_step), current, *held
+            )
+        return current
+
+    onward = [(2 * chip + 1, 2 * chip + 3) for chip in range(1, early - 1)]
     current = lax.fori_loop(
-        0, 2, lambda section, rows: hand_over(when(section, rows, start), [(0, 1), (1, 3)]), latents
-    )
-    own_packed, *first_held = lax.cond(
-        section_index >= 2, chip_sections, unused(chip_sections), own_weights, aux, mod
-    )
-    own_packed, first_packed = pl.pallas_call(
-        nothing_kernel,
-        out_shape=(jax.ShapeDtypeStruct(own_packed.shape, BF16),) * 2,
-        in_specs=[ANY] * 2,
-        out_specs=(ANY,) * 2,
-        input_output_aliases={0: 0, 1: 1},
-        name="pass_on",
-    )(own_packed, first_held[0])
-    small = pl.pallas_call(
-        keep_kernel,
-        out_shape=tuple(pltpu.VMEM(value.shape, value.dtype) for value in (aux, mod)),
-        in_specs=[near] + [ANY] * 2,
-        out_specs=(VMEM, VMEM),
-        scratch_shapes=[pltpu.SemaphoreType.DMA((2,))],
-        compiler_params=LARGE,
-        name="keep",
-    )(section_index.astype(jnp.int32).reshape(1), *first_held[1:])
-    first_held = (first_packed, *small)
-    second_held = (own_packed, aux, mod)
-    last = section_count // 2 - 1
-    onward = [[(2 * c + 1, 2 * c + 3) for c in range(first, last, 2)] for first in (1, 2)]
-
-    def two_chips(turn, current):
-        for i, pairs in enumerate(onward):
-            current = hand_over(chip_turn(2 * turn + 1 + i, current), pairs)
-        return current
-
-    current = lax.fori_loop(0, last // 2, two_chips, current)
-    current = chip_turn(last, current)
-    pieces = current.reshape(own_rows, section_count, width // section_count).swapaxes(0, 1)
-    pieces = lax.all_to_all(pieces, "section", split_axis=0, concat_axis=0, tiled=True)
-    return pieces[section_count - 1]
+        1, early - 1, lambda chip, rows: hand_over(turn(chip, rows), onward), current
+    )
+    current = turn(early - 1, current)
+
+    current = pl.pallas_call(
+        same_kernel,
+        out_shape=pltpu.VMEM(current.shape, BF16),
+        in_specs=[VMEM],
+        out_specs=VMEM,
+        compiler_params=PARAMS,
+        name="rows_so_far",
+    )(current)
+
+    def from_owners(value, step):
+        received = []
+        for half in range(2):
+            pairs = []
+            for seat in range(8):
+                owner = (half * SECOND + seat * HELD) // own_rows + step
+                pairs.append(
+                    (
+                        (2 * early - 1) * req_count + owner,
+                        (2 * early + 1) * req_count + 8 * half + seat,
+                    )
+                )
+            received.append(lax.ppermute(value, AXES, pairs))
+        return jnp.where(req_index < 8, received[0], received[1])
+
+    current = pl.pallas_call(
+        fold_kernel,
+        out_shape=jax.ShapeDtypeStruct(folded, BF16),
+        in_specs=[near, VMEM, VMEM],
+        out_specs=VMEM,
+        compiler_params=PARAMS,
+        name="fold_rows",
+    )(req_id, from_owners(current, 0), from_owners(current, 1))
+    onward_late = [
+        [(2 * chip + 1, 2 * chip + 3) for chip in range(first, section_count // 2 - 1, 2)]
+        for first in (early, early + 1)
+    ]
+
+    def two_late_chips(step, current):
+        chip = early + 2 * step
+        current = hand_over(late_turn(chip, current), onward_late[0])
+        current = late_turn(chip + 1, current)
+        return jnp.where(
+            section_index == section_count - 1, current, hand_over(current, onward_late[1])
+        )
+
+    current = lax.fori_loop(0, (section_count // 2 - early) // 2, two_late_chips, current)
+    rows = pl.pallas_call(
+        unfold_kernel,
+        out_shape=jax.ShapeDtypeStruct((16, width), BF16),
+        in_specs=[VMEM],
+        out_specs=VMEM,
+        compiler_params=PARAMS,
+        name="unfold_rows",
+    )(current)
+    columns = width // section_count
+    rows = rows.reshape(16, section_count, columns).swapaxes(0, 1)
+    rows = lax.all_to_all(rows, "section", split_axis=0, concat_axis=0, tiled=True)
+    placed = pl.pallas_call(
+        place_kernel,
+        out_shape=jax.ShapeDtypeStruct((patches, columns), BF16),
+        in_specs=[near, VMEM, VMEM],
+        out_specs=VMEM,
+        compiler_params=PARAMS,
+        name="place_rows",
+    )(req_id, rows[section_count - 1], request_len.reshape(1, -1))
+    placed = placed.reshape(req_count, own_rows, columns)
+    placed = lax.all_to_all(placed, "req", split_axis=0, concat_axis=0, tiled=True)
+    return jnp.sum(placed.astype(jnp.float32), axis=0).astype(BF16)
 
 
 def solution(mesh):

time: 507 us -> 505 us (level)
  waiting for transfers between devices: 11.3 us -> 40.2 us
  starting transfers between devices: 34.9 us -> 9.37 us
  blocking collectives: 453 us -> 442 us
    ppermute x8, waiting for transfers between devices: 11.3 us -> 40.2 us  [hand_over(): return lax.ppermute(current, AXES, pairs)]
    ppermute x8, starting transfers between devices: 34.9 us -> 6.71 us  [hand_over(): return lax.ppermute(current, AXES, pairs)]
    all_to_all x1 -> x2, blocking collectives: 427 us -> 416 us  [the longest x1 407 us: shards(): lax.all_to_all(rows, 'section', split_axis=0, concat_axis=0, tiled=True)]
  transfers between devices with their start and end apart: 8 -> 12, of which waited for: 2 -> 2; matrix products, arithmetic and copies ran while one was open for 0% -> 0% of each run, Pallas kernels for 0% -> 0%
where the time goes in v5:
time: 505 us
  blocking collectives  442 us (88%)
  waiting for transfers between devices  40.2 us (8%)
  starting transfers between devices  9.37 us (2%)
  Pallas kernels  7.29 us (1%)
    all_to_all x1, blocking collectives, shards(): lax.all_to_all(rows, 'section', split_axis=0, concat_axis=0, tiled=True)  407 us
    ppermute x8, waiting for transfers between devices, hand_over(): return lax.ppermute(current, AXES, pairs)  40.2 us
    all_to_all x2, blocking collectives, exchange(): lax.all_to_all(value, 'req', split_axis=0, concat_axis=0, tiled=True)  26.2 us
  transfers between devices with their start and end apart: 12, of which 2 were waited for; matrix products, arithmetic and copies ran while one was open for 0% of the time, Pallas kernels for 0%

profile of v5, /device:TPU:1, one launch (start us, length us, event | category | flops | bytes accessed | tf_op | source)
XLA Modules:
  0.0 504.7 jit_solution(5198544680234086925)
XLA Ops:
  0.0 1.8 prepare.1
  1.9 0.0 copy-start.10
  1.9 0.0 copy-start.15
  1.9 1.6 copy-done.10
  3.5 0.2 copy-done.15
  3.7 0.0 copy-start.27
  3.7 0.0 copy-start.29
  3.7 0.6 copy-done.27
  4.4 0.0 copy-done.29
  4.4 0.0 copy-done.30
  4.4 1.3 collective-permute-start.13
  5.7 38.9 %collective-permute-done.13 = bf16[8,3072]{1,0:T(8,128)(2,1)} collective-permute-done((bf16[8,3072]{1,0:T(8,128)(2,1)}, bf16[8,3072]{1,0:T(8,128)(2,1)}, u32[]{:S(2)}, u32[]{:S(2)}) %collective-permute-start.13) | collective-permute-done | bytes 49184 | tf_op jit(solution)/shard_map/ppermute | solution.py:615
  44.6 31.0 %conditional.13 = (bf16[8,3072]{1,0:T(8,128)(2,1)}) conditional(s32[]{:T(128)} %convert_element_type.49, () %tuple.118, (bf16[8,3072]{1,0:T(8,128)(2,1)}, f32[3,8,3072]{2,1,0:T(8,128)S(1)}, bf16[3072,384]{1,0:T(8,128)(2,1)S(1)}, bf16[3072,384]{1,0:T(8,128)(2,1)}, bf16[128,3072]{1,0:T(8,128)(2,1)S(1)}, /*index=5*/bf16[384,3072]{1,0:T(8,128)(2,1)}, ...), branch_computations={%region_2.0_spmd, %region_3.0_spmd} | conditional | bytes 22020160 | solution.py:609
  44.6 1.2 spread_normed.7
  45.9 13.1 %all_to_all.92 = bf16[16,8,3072]{2,1,0:T(8,128)(2,1)S(1)} all-to-all(bf16[16,8,3072]{2,1,0:T(8,128)(2,1)S(1)} %bitcast.103), channel_id=1, replica_groups=mesh['section'=16,'req'=16] {'req'}, dimensions={0} | all-to-all | bytes 1572864 | tf_op jit(solution)/shard_map/cond/branch_1_fun/all_to_all | solution.py:599
  59.0 0.0 copy-done.12
  59.0 0.0 copy-done.14
  59.0 2.1 heads_and_units.7
  61.1 13.0 %all_to_all.93 = bf16[16,8,3072]{2,1,0:T(8,128)(2,1)S(1)} all-to-all(bf16[16,8,3072]{2,1,0:T(8,128)(2,1)S(1)} %bitcast.97), channel_id=1, replica_groups=mesh['section'=16,'req'=16] {'req'}, dimensions={0} | all-to-all | bytes 1572864 | tf_op jit(solution)/shard_map/cond/branch_1_fun/all_to_all | solution.py:599
  74.1 1.5 add_shares.7
  75.6 1.5 collective-permute-start.14
  77.1 1.3 collective-permute-done.14
  78.4 1.4 while.28
  78.4 0.7 collective-permute-start.10
  79.0 0.0 collective-permute-done.10
  79.1 0.7 collective-permute-start.10
  79.8 0.0 collective-permute-done.10
  79.9 0.7 collective-permute-start.18
  80.6 0.7 collective-permute-start.17
  81.2 0.0 copy-start.17
  81.3 0.0 copy-start.20
  81.3 0.0 copy-start.22
  81.3 0.0 copy-start.24
  81.3 0.0 copy-start.26
  81.3 0.9 copy-done.17
  82.2 0.0 copy-done.20
  82.2 0.0 copy-done.22
  82.2 0.0 copy-done.24
  82.2 0.0 copy-done.26
  82.3 0.1 keep.3
  82.3 0.7 collective-permute-start.16
  83.0 0.7 collective-permute-start.15
  83.7 0.0 collective-permute-done.18
  83.7 0.0 collective-permute-done.17
  83.7 0.0 collective-permute-done.16
  83.7 0.0 collective-permute-done.15
  83.8 0.2 fold_rows.1
  84.0 0.0 copy-start.28
  84.0 3.3 while.29
  84.3 0.7 collective-permute-start.11
  84.9 0.0 collective-permute-done.11
  85.0 0.7 collective-permute-start.12
  85.7 0.0 collective-permute-done.12
  85.8 0.7 collective-permute-start.11
  86.5 0.0 collective-permute-done.11
  86.6 0.7 collective-permute-start.12
  87.2 0.0 collective-permute-done.12
  87.3 0.1 unfold_rows.1
  87.3 0.2 reshape.145
  87.6 406.6 %all_to_all.110 = bf16[16,16,192]{2,1,0:T(8,128)(2,1)S(1)} all-to-all(bf16[16,16,192]{2,1,0:T(8,128)(2,1)S(1)} %bitcast.113), channel_id=1, replica_groups=mesh['section'=16,'req'=16] {'section'}, dimensions={0} | all-to-all | bytes 196608 | tf_op jit(solution)/shard_map/all_to_all | solution.py:821
  494.2 0.0 copy-done.28
  494.2 0.3 place_rows.1
  494.5 9.5 %all_to_all.111 = bf16[16,8,192]{2,1,0:T(8,128)(2,1)S(1)} all-to-all(bf16[16,8,192]{2,1,0:T(8,128)(2,1)S(1)} %bitcast.110), channel_id=1, replica_groups=mesh['section'=16,'req'=16] {'req'}, dimensions={0} | all-to-all | bytes 98304 | tf_op jit(solution)/shard_map/all_to_all | solution.py:831
  504.1 0.6 reduce_sum.12
  (47 shorter events, 0.4 us)
Async XLA Ops:
  1.9 1.7 copy-start.10
  1.9 1.8 copy-start.15
  3.7 0.7 copy-start.27
  3.7 0.7 copy-start.29
  3.7 0.7 copy-start.30
  4.4 40.2 %collective-permute-start.13 = (bf16[8,3072]{1,0:T(8,128)(2,1)}, bf16[8,3072]{1,0:T(8,128)(2,1)}, u32[]{:S(2)}, u32[]{:S(2)}) collective-permute-start(bf16[8,3072]{1,0:T(8,128)(2,1)} %get-tuple-element.1103), channel_id=1, source_target_pairs={{0,16},{1,17},{2,18},{3,19},{4,20},{5,21},{6,22},{7,23},{8,24},{9,... | collective-permute-start | bytes 147464 | tf_op jit(solution)/shard_map/ppermute | solution.py:615
  44.6 14.4 %copy-start.12 = (bf16[3072,384]{1,0:T(8,128)(2,1)S(1)}, bf16[3072,384]{1,0:T(8,128)(2,1)}, u32[]{:S(2)}) copy-start(bf16[3072,384]{1,0:T(8,128)(2,1)} %get-tuple-element.658.refs_1_.mlp_ref) | copy-start | bytes 7077892 | tf_op jit(solution)/shard_map/cond
  44.6 14.4 %copy-start.14 = (bf16[384,3072]{1,0:T(8,128)(2,1)S(1)}, bf16[384,3072]{1,0:T(8,128)(2,1)}, u32[]{:S(2)}) copy-start(bf16[384,3072]{1,0:T(8,128)(2,1)} %get-tuple-element.660.refs_3_.mlp_out_ref) | copy-start | bytes 7077892 | tf_op jit(solution)/shard_map/cond
  75.6 2.8 collective-permute-start.14
  78.4 0.7 collective-permute-start.10
  79.1 0.7 collective-permute-start.10
  79.9 3.8 collective-permute-start.18
  80.6 3.1 collective-permute-start.17
  81.2 1.0 copy-start.17
  81.3 1.0 copy-start.20
  81.3 1.0 copy-start.22
  81.3 1.0 copy-start.24
  81.3 1.0 copy-start.26
  82.3 1.4 collective-permute-start.16
  83.0 0.7 collective-permute-start.15
  84.0 410.3 %copy-start.28 = (s32[16]{0:T(128)S(1)}, s32[16]{0:T(128)}, u32[]{:S(2)}) copy-start(s32[16]{0:T(128)} %param.40) | copy-start | bytes 196
  84.3 0.7 collective-permute-start.11
  85.0 0.7 collective-permute-start.12
  85.8 0.7 collective-permute-start.11
  86.6 0.7 collective-permute-start.12

commit v6 on v5

--- a/solution.py
+++ b/solution.py
@@ -383,18 +383,17 @@
                     [spread_ref[k * tiles + t, pl.ds(s, 8, stride=8), :] for k in (i, i + 1)],
                     axis=0,
                 ).astype(BF16)
-    sums = [
-        jnp.dot(inputs_ref[...], packed_ref[:width, :], preferred_element_type=jnp.float32)
-    ]
+    def inner_of(weights, extra):
+        sums = jnp.dot(
+            inputs_ref[...], weights[:width, :], preferred_element_type=jnp.float32
+        )
+        attended = attend(sums[:, :qkv_cols].astype(BF16), extra)
+        mlp_act = gelu_tanh(sums[:, qkv_cols:]).astype(BF16)
+        return jnp.concatenate([attended, mlp_act], axis=1)
+
+    inner = [inner_of(packed_ref, aux_ref)]
     reads[0].wait()
-    sums.append(
-        jnp.dot(inputs_ref[...], their_packed_ref[:width, :], preferred_element_type=jnp.float32)
-    )
-    inner = []
-    for values, extra in zip(sums, (aux_ref, their_aux_ref)):
-        attended = attend(values[:, :qkv_cols].astype(BF16), extra)
-        mlp_act = gelu_tanh(values[:, qkv_cols:]).astype(BF16)
-        inner.append(jnp.concatenate([attended, mlp_act], axis=1))
+    inner.append(inner_of(their_packed_ref, their_aux_ref))
     reads[1].wait()
     for cut in range(cuts):
         first = width + cut * depth

time: 505 us -> 503 us (level)
  no operation moved by 1% of the time
where the time goes in v6:
time: 503 us
  blocking collectives  440 us (87%)
  waiting for transfers between devices  40.2 us (8%)
  starting transfers between devices  9.37 us (2%)
  Pallas kernels  7.29 us (1%)
    all_to_all x1, blocking collectives, shards(): lax.all_to_all(rows, 'section', split_axis=0, concat_axis=0, tiled=True)  405 us
    ppermute x8, waiting for transfers between devices, hand_over(): return lax.ppermute(current, AXES, pairs)  40.2 us
    all_to_all x2, blocking collectives, exchange(): lax.all_to_all(value, 'req', split_axis=0, concat_axis=0, tiled=True)  26.2 us
  transfers between devices with their start and end apart: 12, of which 2 were waited for; matrix products, arithmetic and copies ran while one was open for 0% of the time, Pallas kernels for 0%

profile of v6, /device:TPU:1, one launch (start us, length us, event | category | flops | bytes accessed | tf_op | source)
XLA Modules:
  0.0 502.5 jit_solution(4223124465841796112)
XLA Ops:
  0.0 1.8 prepare.1
  1.9 0.0 copy-start.10
  1.9 0.0 copy-start.15
  1.9 1.6 copy-done.10
  3.5 0.2 copy-done.15
  3.7 0.0 copy-start.27
  3.7 0.0 copy-start.29
  3.7 0.6 copy-done.27
  4.4 0.0 copy-done.29
  4.4 0.0 copy-done.30
  4.4 1.3 collective-permute-start.13
  5.7 38.9 %collective-permute-done.13 = bf16[8,3072]{1,0:T(8,128)(2,1)} collective-permute-done((bf16[8,3072]{1,0:T(8,128)(2,1)}, bf16[8,3072]{1,0:T(8,128)(2,1)}, u32[]{:S(2)}, u32[]{:S(2)}) %collective-permute-start.13) | collective-permute-done | bytes 49184 | tf_op jit(solution)/shard_map/ppermute | solution.py:614
  44.6 31.0 %conditional.13 = (bf16[8,3072]{1,0:T(8,128)(2,1)}) conditional(s32[]{:T(128)} %convert_element_type.49, () %tuple.118, (bf16[8,3072]{1,0:T(8,128)(2,1)}, f32[3,8,3072]{2,1,0:T(8,128)S(1)}, bf16[3072,384]{1,0:T(8,128)(2,1)S(1)}, bf16[3072,384]{1,0:T(8,128)(2,1)}, bf16[128,3072]{1,0:T(8,128)(2,1)S(1)}, /*index=5*/bf16[384,3072]{1,0:T(8,128)(2,1)}, ...), branch_computations={%region_2.0_spmd, %region_3.0_spmd} | conditional | bytes 22020160 | solution.py:608
  44.6 1.2 spread_normed.7
  45.9 13.1 %all_to_all.92 = bf16[16,8,3072]{2,1,0:T(8,128)(2,1)S(1)} all-to-all(bf16[16,8,3072]{2,1,0:T(8,128)(2,1)S(1)} %bitcast.103), channel_id=1, replica_groups=mesh['section'=16,'req'=16] {'req'}, dimensions={0} | all-to-all | bytes 1572864 | tf_op jit(solution)/shard_map/cond/branch_1_fun/all_to_all | solution.py:598
  59.0 0.0 copy-done.12
  59.0 0.0 copy-done.14
  59.0 2.1 heads_and_units.7
  61.1 13.0 %all_to_all.93 = bf16[16,8,3072]{2,1,0:T(8,128)(2,1)S(1)} all-to-all(bf16[16,8,3072]{2,1,0:T(8,128)(2,1)S(1)} %bitcast.97), channel_id=1, replica_groups=mesh['section'=16,'req'=16] {'req'}, dimensions={0} | all-to-all | bytes 1572864 | tf_op jit(solution)/shard_map/cond/branch_1_fun/all_to_all | solution.py:598
  74.1 1.5 add_shares.7
  75.6 1.5 collective-permute-start.14
  77.1 1.3 collective-permute-done.14
  78.4 1.4 while.28
  78.4 0.7 collective-permute-start.10
  79.0 0.0 collective-permute-done.10
  79.1 0.7 collective-permute-start.10
  79.8 0.0 collective-permute-done.10
  79.9 0.7 collective-permute-start.18
  80.6 0.7 collective-permute-start.17
  81.2 0.0 copy-start.17
  81.3 0.0 copy-start.20
  81.3 0.0 copy-start.22
  81.3 0.0 copy-start.24
  81.3 0.0 copy-start.26
  81.3 0.9 copy-done.17
  82.2 0.0 copy-done.20
  82.2 0.0 copy-done.22
  82.2 0.0 copy-done.24
  82.2 0.0 copy-done.26
  82.3 0.1 keep.3
  82.3 0.7 collective-permute-start.16
  83.0 0.7 collective-permute-start.15
  83.7 0.0 collective-permute-done.18
  83.7 0.0 collective-permute-done.17
  83.7 0.0 collective-permute-done.16
  83.7 0.0 collective-permute-done.15
  83.8 0.2 fold_rows.1
  84.0 0.0 copy-start.28
  84.0 3.3 while.29
  84.3 0.7 collective-permute-start.11
  84.9 0.0 collective-permute-done.11
  85.0 0.7 collective-permute-start.12
  85.7 0.0 collective-permute-done.12
  85.8 0.7 collective-permute-start.11
  86.5 0.0 collective-permute-done.11
  86.6 0.7 collective-permute-start.12
  87.2 0.0 collective-permute-done.12
  87.3 0.1 unfold_rows.1
  87.3 0.2 reshape.145
  87.6 404.5 %all_to_all.110 = bf16[16,16,192]{2,1,0:T(8,128)(2,1)S(1)} all-to-all(bf16[16,16,192]{2,1,0:T(8,128)(2,1)S(1)} %bitcast.113), channel_id=1, replica_groups=mesh['section'=16,'req'=16] {'section'}, dimensions={0} | all-to-all | bytes 196608 | tf_op jit(solution)/shard_map/all_to_all | solution.py:820
  492.1 0.0 copy-done.28
  492.1 0.3 place_rows.1
  492.4 9.5 %all_to_all.111 = bf16[16,8,192]{2,1,0:T(8,128)(2,1)S(1)} all-to-all(bf16[16,8,192]{2,1,0:T(8,128)(2,1)S(1)} %bitcast.110), channel_id=1, replica_groups=mesh['section'=16,'req'=16] {'req'}, dimensions={0} | all-to-all | bytes 98304 | tf_op jit(solution)/shard_map/all_to_all | solution.py:830
  501.9 0.6 reduce_sum.12
  (47 shorter events, 0.4 us)
Async XLA Ops:
  1.9 1.7 copy-start.10
  1.9 1.8 copy-start.15
  3.7 0.7 copy-start.27
  3.7 0.7 copy-start.29
  3.7 0.7 copy-start.30
  4.4 40.2 %collective-permute-start.13 = (bf16[8,3072]{1,0:T(8,128)(2,1)}, bf16[8,3072]{1,0:T(8,128)(2,1)}, u32[]{:S(2)}, u32[]{:S(2)}) collective-permute-start(bf16[8,3072]{1,0:T(8,128)(2,1)} %get-tuple-element.1103), channel_id=1, source_target_pairs={{0,16},{1,17},{2,18},{3,19},{4,20},{5,21},{6,22},{7,23},{8,24},{9,... | collective-permute-start | bytes 147464 | tf_op jit(solution)/shard_map/ppermute | solution.py:614
  44.6 14.4 %copy-start.12 = (bf16[3072,384]{1,0:T(8,128)(2,1)S(1)}, bf16[3072,384]{1,0:T(8,128)(2,1)}, u32[]{:S(2)}) copy-start(bf16[3072,384]{1,0:T(8,128)(2,1)} %get-tuple-element.658.refs_1_.mlp_ref) | copy-start | bytes 7077892 | tf_op jit(solution)/shard_map/cond
  44.6 14.4 %copy-start.14 = (bf16[384,3072]{1,0:T(8,128)(2,1)S(1)}, bf16[384,3072]{1,0:T(8,128)(2,1)}, u32[]{:S(2)}) copy-start(bf16[384,3072]{1,0:T(8,128)(2,1)} %get-tuple-element.660.refs_3_.mlp_out_ref) | copy-start | bytes 7077892 | tf_op jit(solution)/shard_map/cond
  75.6 2.8 collective-permute-start.14
  78.4 0.7 collective-permute-start.10
  79.1 0.7 collective-permute-start.10
  79.9 3.8 collective-permute-start.18
  80.6 3.1 collective-permute-start.17
  81.2 1.0 copy-start.17
  81.3 1.0 copy-start.20
  81.3 1.0 copy-start.22
  81.3 1.0 copy-start.24
  81.3 1.0 copy-start.26
  82.3 1.4 collective-permute-start.16
  83.0 0.7 collective-permute-start.15
  84.0 408.2 %copy-start.28 = (s32[16]{0:T(128)S(1)}, s32[16]{0:T(128)}, u32[]{:S(2)}) copy-start(s32[16]{0:T(128)} %param.40) | copy-start | bytes 196
  84.3 0.7 collective-permute-start.11
  85.0 0.7 collective-permute-start.12
  85.8 0.7 collective-permute-start.11
  86.6 0.7 collective-permute-start.12
